TPU v7x, 256 devices: a whole 4x4x8 slice. The times are simulated.
256 devices in a mesh: dp: 4 (over y), expert: 64 (over x, z, core).
Axes of the slice: x: 4, y: 4, z: 8, core: 2. Of those that a mesh axis runs over, the one named last changes fastest.
Arguments:
- tokens: bfloat16 [32768, 2048], P(('dp', 'expert')), parts along dimension 0, may hold values from -6 to 6
- cotangent: bfloat16 [32768, 2048], P(('dp', 'expert')), parts along dimension 0, may hold values from -6 to 6
- routes: int32 [32768, 8], P(('dp', 'expert')), parts along dimension 0, may hold values from 0 to 63, all different within a row; in each aligned block of 128 rows (0 to 127, 128 to 255, ...) at most 18 rows name the same one
- route_weight: float32 [32768, 8], P(('dp', 'expert')), parts along dimension 0, may hold values from 0.1 to 1
- example_ids: int32 [32768], P(('dp', 'expert')), parts along dimension 0, may hold values from 0 to 1
- w_gate: bfloat16 [64, 2048, 768], P('expert'), may hold values from -0.125 to 0.125
- w_up: bfloat16 [64, 2048, 768], P('expert'), may hold values from -0.125 to 0.125
- w_down: bfloat16 [64, 768, 2048], P('expert'), may hold values from -0.21875 to 0.21875
- proj_model: bfloat16 [64, 2048], replicated, may hold values from -0.125 to 0.125
- proj_hidden: bfloat16 [64, 768], replicated, may hold values from -0.21875 to 0.21875
Outputs:
- proj_grads: bfloat16 [512, 64, 2, 4096], P(('dp', 'expert')), parts along dimension 0
There are 4 independent parts, one for each index of `dp`. A program takes and returns all parts, laid end to end along the dimension named above; an argument that names none is the same for every part. Nothing has to cross between parts.
Inputs may be any that keep to these rules, and one draw needn't show every extreme that they name: `routes`: each token names 8 different experts; among the rows of one device at most 18 name any one expert.
All inputs are finite; a program needn't handle non-finite values.
Results may differ from a plain program's by a relative error of at most 0.007.
Values may be sent and summed in bfloat16 or wider, within the bound.
No kernel may reach another device: no remote copies, remote signals or barrier semaphores. Data moves between devices by JAX's collectives and lax.ppermute only.
A program may use at most 128 MiB of HBM per device.

v0:
```python
import jax
import jax.numpy as jnp
from jax import lax
from jax.sharding import PartitionSpec as P

EX_DEV = 2


def project(rows, proj):
    return jnp.einsum("...d,rd->...r", rows, proj, preferred_element_type=jnp.float32).astype(
        jnp.bfloat16
    )


def shards(
    tokens,
    cotangent,
    routes,
    route_weight,
    example_ids,
    w_gate,
    w_up,
    w_down,
    proj_model,
    proj_hidden,
):
    experts = lax.axis_size("expert")
    tok_dev, width = tokens.shape
    top = routes.shape[1]
    rank_dim = proj_model.shape[0]
    cap = min(tok_dev, tok_dev * top // experts + 2)
    count = tok_dev * top
    flat_e = routes.reshape(-1)
    onehot = (flat_e[:, None] == jnp.arange(experts, dtype=jnp.int32)[None, :]).astype(jnp.int32)
    rank = jnp.sum((jnp.cumsum(onehot, axis=0) - onehot) * onehot, axis=1)
    table = jnp.full((experts * cap,), count, jnp.int32)
    table = table.at[flat_e * cap + rank].set(jnp.arange(count, dtype=jnp.int32))
    valid = table < count
    safe = jnp.minimum(table, count - 1)
    tok = safe // top
    send_x = jnp.where(valid[:, None], tokens[tok], jnp.zeros((), tokens.dtype))
    wslot = jnp.where(valid, route_weight.reshape(-1)[safe], 0.0)
    send_dg = (wslot[:, None] * cotangent[tok].astype(jnp.float32)).astype(jnp.bfloat16)
    member = (
        (example_ids[tok][:, None] == jnp.arange(EX_DEV, dtype=jnp.int32)[None, :]) & valid[:, None]
    ).astype(jnp.bfloat16)
    gate_w = w_gate[0]
    up_w = w_up[0]
    down_w = w_down[0]
    xs_slots = send_x.reshape(experts, cap, width)
    dg_slots = send_dg.reshape(experts, cap, width)
    member_slots = member.reshape(experts, cap, EX_DEV)
    recv_x, recv_dg, recv_member = (
        lax.all_to_all(xs_slots, "expert", split_axis=0, concat_axis=0, tiled=True),
        lax.all_to_all(dg_slots, "expert", split_axis=0, concat_axis=0, tiled=True),
        lax.all_to_all(member_slots, "expert", split_axis=0, concat_axis=0, tiled=True),
    )
    lead = recv_x.shape[:2]
    xrows = recv_x.reshape(-1, recv_x.shape[2])
    dgrows = recv_dg.reshape(-1, recv_dg.shape[2])
    gate = jnp.dot(xrows, gate_w, preferred_element_type=jnp.float32)
    upval = jnp.dot(xrows, up_w, preferred_element_type=jnp.float32)
    sig = jax.nn.sigmoid(gate)
    hidden = (gate * sig * upval).astype(jnp.bfloat16)
    back = lax.dot_general(
        dgrows, down_w, (((1,), (1,)), ((), ())), preferred_element_type=jnp.float32
    )
    delta = (back * upval * sig * (1.0 + gate * (1.0 - sig))).astype(jnp.bfloat16)
    joined = jnp.concatenate([project(hidden, proj_hidden), project(delta, proj_hidden)], axis=1)
    joined = joined.reshape(lead + (2 * rank_dim,))
    in_model = project(recv_x, proj_model)
    out_model = project(recv_dg, proj_model)
    lhs_gate = recv_member[:, :, :, None] * in_model[:, :, None, :]
    lhs_down = recv_member[:, :, :, None] * joined[:, :, None, :rank_dim]
    gate_blk = jnp.einsum(
        "ncsi,ncj->snij", lhs_gate, joined[:, :, rank_dim:], preferred_element_type=jnp.float32
    )
    down_blk = jnp.einsum("ncsi,ncj->snij", lhs_down, out_model, preferred_element_type=jnp.float32)
    shape_out = gate_blk.shape[:2] + (rank_dim * rank_dim,)
    blocks = jnp.stack([gate_blk.reshape(shape_out), down_blk.reshape(shape_out)], axis=2).astype(
        jnp.bfloat16
    )
    return lax.all_to_all(blocks, "expert", split_axis=1, concat_axis=1, tiled=True)


def solution(mesh):
    placed = (
        P(("dp", "expert"), None),
        P(("dp", "expert"), None),
        P(("dp", "expert"), None),
        P(("dp", "expert"), None),
        P(("dp", "expert")),
        P("expert", None, None),
        P("expert", None, None),
        P("expert", None, None),
        P(),
        P(),
    )
    return jax.shard_map(
        shards,
        mesh=mesh,
        in_specs=placed,
        out_specs=P(("dp", "expert"), None, None, None),
        check_vma=False,
    )
```

profile of v0, /device:TPU:1, one launch (start us, length us, event | category | flops | bytes accessed | tf_op | source)
XLA Modules:
  0.0 498.9 jit_solution(894626912150457686)
XLA Ops:
  2.9 31.1 %reduce-window.6 = s32[64,8,128]{2,1,0:T(8,128)S(1)} reduce-window(s32[64,8,128]{2,1,0:T(8,128)} %fusion.35, s32[]{:T(128)} %constant.15.clone.1), window={size=1x1x128 pad=0_0x0_0x127_0}, to_apply=%region_0.0 | reduce-window | flops 8323072 | bytes 524292 | tf_op jit(solution)/shard_map/reduce-window
  36.3 4.3 scatter_custom_fusion
  41.5 4.6 gather_fusion.1
  46.1 11.8 %gather_fusion = bf16[1152,2048]{1,0:T(8,128)(2,1)} fusion(bf16[128,2048]{1,0:T(8,128)(2,1)} %param.10, s32[2048]{0:T(1024)S(1)} %get-tuple-element.10), kind=kCustom, calls=%fused_computation | custom fusion | bytes 9441792 | tf_op jit(solution)/shard_map/gather | solution.py:41
  57.9 7.6 %gather.15 = bf16[64,18,2048]{2,1,0:T(8,128)(2,1)} reshape(bf16[1152,2048]{1,0:T(8,128)(2,1)} %gather_fusion) | data formatting | bytes 9437184 | tf_op jit(solution)/shard_map/gather | solution.py:41
  65.7 5.9 %broadcast_select_fusion = bf16[64,18,2048]{2,1,0:T(8,128)(2,1)} fusion(bf16[64,18,2048]{2,1,0:T(8,128)(2,1)} %gather.15, pred[64,18]{1,0:T(8,128)(4,1)S(1)} %broadcast_in_dim.22), kind=kLoop, calls=%fused_computation.6 | loop fusion | flops 2359296 | bytes 9438336 | tf_op jit(solution)/shard_map/jit(_where)/select_n | solution.py:41
  71.6 13.2 %all-to-all-start = ((bf16[64,18,2048]{2,1,0:T(8,128)(2,1)}), bf16[64,18,2048]{2,1,0:T(8,128)(2,1)}, u32[]{:S(2)}, u32[]{:S(2)}) async-start(bf16[64,18,2048]{2,1,0:T(8,128)(2,1)} %broadcast_select_fusion), calls=%async_computation | async-start | bytes 12582912 | tf_op jit(solution)/shard_map/all_to_all | solution.py:54
  84.8 11.8 %gather_fusion.2 = bf16[1152,2048]{1,0:T(8,128)(2,1)} fusion(bf16[128,2048]{1,0:T(8,128)(2,1)} %param.11, s32[2048]{0:T(1024)S(1)} %get-tuple-element.10), kind=kCustom, calls=%fused_computation.2 | custom fusion | bytes 9441792 | tf_op jit(solution)/shard_map/gather | solution.py:43
  96.5 8.4 %reshape.98 = f32[64,18,2048]{2,1,0:T(8,128)} reshape(bf16[1152,2048]{1,0:T(8,128)(2,1)} %gather_fusion.2) | data formatting | bytes 14155776 | tf_op jit(solution)/shard_map/convert_element_type | solution.py:43
  105.1 7.9 %multiply_convert_fusion = bf16[64,18,2048]{2,1,0:T(8,128)(2,1)} fusion(f32[64,18,2048]{2,1,0:T(8,128)} %reshape.98, f32[64,18]{1,0:T(8,128)S(1)} %mul.78), kind=kLoop, calls=%fused_computation.5 | loop fusion | flops 4718592 | bytes 14160384 | tf_op jit(solution)/shard_map/convert_element_type | solution.py:43
  113.0 112.7 %all-to-all-done = bf16[64,18,2048]{2,1,0:T(8,128)(2,1)} async-done(((bf16[64,18,2048]{2,1,0:T(8,128)(2,1)}), bf16[64,18,2048]{2,1,0:T(8,128)(2,1)}, u32[]{:S(2)}, u32[]{:S(2)}) %all-to-all-start) | async-done | bytes 4718624 | tf_op jit(solution)/shard_map/all_to_all | solution.py:54
  225.6 6.7 %all-to-all-start.1 = ((bf16[64,18,2048]{2,1,0:T(8,128)(2,1)}), bf16[64,18,2048]{2,1,0:T(8,128)(2,1)}, u32[]{:S(2)}, u32[]{:S(2)}) async-start(bf16[64,18,2048]{2,1,0:T(8,128)(2,1)} %multiply_convert_fusion), calls=%async_computation.1 | async-start | bytes 12582912 | tf_op jit(solution)/shard_map/all_to_all | solution.py:55
  232.3 7.0 %gather_fusion.3 = s32[1152]{0:T(1024)S(1)} fusion(s32[128]{0:T(128)S(1)} %copy-done.2, s32[2048]{0:T(1024)S(1)} %get-tuple-element.10), kind=kCustom, calls=%fused_computation.3 | custom fusion | bytes 13824 | tf_op jit(solution)/shard_map/gather | solution.py:45
  240.1 7.7 %reshape.94 = bf16[1152,2048]{1,0:T(8,128)(2,1)} reshape(bf16[64,18,2048]{2,1,0:T(8,128)(2,1)} %all-to-all-done) | data formatting | bytes 9437184 | tf_op jit(solution)/shard_map/reshape | solution.py:59
  247.8 6.0 %fusion.10 = f32[1152,768]{1,0:T(8,128)S(1)} fusion(bf16[1152,2048]{1,0:T(8,128)(2,1)} %reshape.94, bf16[1,2048,768]{2,1,0:T(8,128)(2,1)S(1)} %copy-done), kind=kOutput, calls=%fused_computation.20 | convolution fusion | flops 3623878656 | bytes 11403264 | tf_op jit(solution)/shard_map/dot_general | solution.py:61
  253.8 3.9 fusion.8
  260.7 112.3 %all-to-all-done.1 = bf16[64,18,2048]{2,1,0:T(8,128)(2,1)} async-done(((bf16[64,18,2048]{2,1,0:T(8,128)(2,1)}), bf16[64,18,2048]{2,1,0:T(8,128)(2,1)}, u32[]{:S(2)}, u32[]{:S(2)}) %all-to-all-start.1) | async-done | bytes 4718624 | tf_op jit(solution)/shard_map/all_to_all | solution.py:55
  372.9 6.1 %all-to-all-start.2 = ((bf16[64,18,2]{1,2,0:T(2,128)(2,1)}), bf16[64,18,2]{1,2,0:T(2,128)(2,1)S(1)}, u32[]{:S(2)}, u32[]{:S(2)}) async-start(bf16[64,18,2]{1,2,0:T(2,128)(2,1)} %and_convert_fusion), calls=%async_computation.2 | async-start | bytes 65536 | tf_op jit(solution)/shard_map/all_to_all | solution.py:56
  379.0 7.7 %reshape.96 = bf16[1152,2048]{1,0:T(8,128)(2,1)} reshape(bf16[64,18,2048]{2,1,0:T(8,128)(2,1)} %all-to-all-done.1) | data formatting | bytes 9437184 | tf_op jit(solution)/shard_map/reshape | solution.py:60
  386.7 10.4 %convolution_convert_fusion = bf16[1152,64]{0,1:T(8,128)(2,1)S(1)} fusion(bf16[64,768]{1,0:T(8,128)(2,1)S(1)} %copy-done.8, f32[1152,768]{1,0:T(8,128)} %copy-done.9, f32[1152,768]{1,0:T(8,128)} %copy-done.10, bf16[1152,2048]{1,0:T(8,128)(2,1)} %reshape.96, bf16[1,768,2048]{2,1,0:T(8,128)(2,1)} %param.17), kind=kOutput, calls=%fused_computation.22 | convolution fusion | flops 3746045952 | bytes 15187968 | tf_op jit(solution)/shard_map/...d,rd->...r/dot_general | solution.py:10
  397.1 8.0 %fusion.20 = bf16[64,18,64,1]{2,0,1,3:T(8,128)(2,1)S(1)} fusion(bf16[64,18,2048]{2,1,0:T(8,128)(2,1)} %all-to-all-done.1, bf16[64,2048]{1,0:T(8,128)(2,1)S(1)} %copy-done.7), kind=kOutput, calls=%fused_computation.29 | convolution fusion | flops 302063616 | bytes 5128192 | tf_op jit(solution)/shard_map/...d,rd->...r/dot_general | solution.py:10
  413.5 8.0 %fusion.14 = bf16[64,18,64]{2,0,1:T(8,128)(2,1)S(1)} fusion(bf16[64,18,2048]{2,1,0:T(8,128)(2,1)} %all-to-all-done, bf16[64,2048]{1,0:T(8,128)(2,1)} %param.18), kind=kOutput, calls=%fused_computation.27 | convolution fusion | flops 302063616 | bytes 5128192 | tf_op jit(solution)/shard_map/...d,rd->...r/dot_general | solution.py:10
  433.6 61.4 %all_to_all.20 = bf16[2,64,2,4096]{3,0,2,1:T(2,128)(2,1)S(1)} all-to-all(bf16[2,64,2,4096]{3,0,2,1:T(2,128)(2,1)S(1)} %copy.55), channel_id=1, replica_groups=mesh['dp'=4,'expert'=64] {'expert'}, dimensions={1} | all-to-all | bytes 4194304 | tf_op jit(solution)/shard_map/all_to_all | solution.py:83
  495.0 3.5 copy.56
  (61 shorter events, 30.4 us)
Async XLA Ops:
  0.0 247.8 %copy-start = (bf16[1,2048,768]{2,1,0:T(8,128)(2,1)S(1)}, bf16[1,2048,768]{2,1,0:T(8,128)(2,1)}, u32[]{:S(2)}) copy-start(bf16[1,2048,768]{2,1,0:T(8,128)(2,1)} %param.15) | copy-start | bytes 9437188
  71.6 154.0 %all-to-all-start = ((bf16[64,18,2048]{2,1,0:T(8,128)(2,1)}), bf16[64,18,2048]{2,1,0:T(8,128)(2,1)}, u32[]{:S(2)}, u32[]{:S(2)}) async-start(bf16[64,18,2048]{2,1,0:T(8,128)(2,1)} %broadcast_select_fusion), calls=%async_computation | async-start | bytes 12582912 | tf_op jit(solution)/shard_map/all_to_all | solution.py:54
  113.0 119.3 %copy-start.2 = (s32[128]{0:T(128)S(1)}, s32[128]{0:T(128)}, u32[]{:S(2)}) copy-start(s32[128]{0:T(128)} %param.14) | copy-start | bytes 1540
  225.6 147.3 %all-to-all-start.1 = ((bf16[64,18,2048]{2,1,0:T(8,128)(2,1)}), bf16[64,18,2048]{2,1,0:T(8,128)(2,1)}, u32[]{:S(2)}, u32[]{:S(2)}) async-start(bf16[64,18,2048]{2,1,0:T(8,128)(2,1)} %multiply_convert_fusion), calls=%async_computation.1 | async-start | bytes 12582912 | tf_op jit(solution)/shard_map/all_to_all | solution.py:55
  247.8 6.0 %copy-start.3 = (bf16[1152,2048]{1,0:T(8,128)(2,1)S(1)}, bf16[1152,2048]{1,0:T(8,128)(2,1)}, u32[]{:S(2)}) copy-start(bf16[1152,2048]{1,0:T(8,128)(2,1)} %reshape.94) | copy-start | bytes 14155780
  247.8 6.0 %copy-start.6 = (bf16[1,2048,768]{2,1,0:T(8,128)(2,1)S(1)}, bf16[1,2048,768]{2,1,0:T(8,128)(2,1)}, u32[]{:S(2)}) copy-start(bf16[1,2048,768]{2,1,0:T(8,128)(2,1)} %param.16) | copy-start | bytes 9437188
  253.8 3.9 copy-start.9
  253.8 5.7 %copy-start.8 = (bf16[64,768]{1,0:T(8,128)(2,1)S(1)}, bf16[64,768]{1,0:T(8,128)(2,1)}, u32[]{:S(2)}) copy-start(bf16[64,768]{1,0:T(8,128)(2,1)} %param.19) | copy-start | bytes 294916
  257.7 1.8 copy-start.10
  372.9 32.5 %all-to-all-start.2 = ((bf16[64,18,2]{1,2,0:T(2,128)(2,1)}), bf16[64,18,2]{1,2,0:T(2,128)(2,1)S(1)}, u32[]{:S(2)}, u32[]{:S(2)}) async-start(bf16[64,18,2]{1,2,0:T(2,128)(2,1)} %and_convert_fusion), calls=%async_computation.2 | async-start | bytes 65536 | tf_op jit(solution)/shard_map/all_to_all | solution.py:56
  386.7 10.4 %copy-start.7 = (bf16[64,2048]{1,0:T(8,128)(2,1)S(1)}, bf16[64,2048]{1,0:T(8,128)(2,1)}, u32[]{:S(2)}) copy-start(bf16[64,2048]{1,0:T(8,128)(2,1)} %param.18) | copy-start | bytes 786436
  405.5 0.6 copy-start.4
  413.5 8.3 %copy-start.5 = (bf16[64,18,2]{1,2,0:T(2,128)(2,1)S(1)}, bf16[64,18,2]{1,2,0:T(2,128)(2,1)}, u32[]{:S(2)}) copy-start(bf16[64,18,2]{1,2,0:T(2,128)(2,1)} %copy-done.4) | copy-start | bytes 13828
  431.4 67.1 %copy-start.1 = (bf16[1,2048,768]{2,1,0:T(8,128)(2,1)S(1)}, bf16[1,2048,768]{2,1,0:T(8,128)(2,1)}, u32[]{:S(2)}) copy-start(bf16[1,2048,768]{2,1,0:T(8,128)(2,1)} %param.15) | copy-start | bytes 9437188
where the time goes:
time: 509 us; the launch traced here: 499 us
  waiting for transfers between devices  225 us (44%)
  local copies, waits for them, and re-layouts  94.6 us (19%)
  blocking collectives  61.4 us (12%)
  other arithmetic  48.9 us (10%)
  matrix products  42.4 us (8%)
  starting transfers between devices  25.9 us (5%)
    all_to_all x1, waiting for transfers between devices, shards(): lax.all_to_all(xs_slots, 'expert', split_axis=0, concat_axis=0, tiled=True)  113 us
    all_to_all x1, waiting for transfers between devices, shards(): lax.all_to_all(dg_slots, 'expert', split_axis=0, concat_axis=0, tiled=True)  112 us
    all_to_all x1, blocking collectives, shards(): lax.all_to_all(blocks, 'expert', split_axis=1, concat_axis=1, tiled=True)  61.4 us
    another operation x3, other arithmetic  31.3 us
    dot_general x4, matrix products, project(): jnp.einsum('...d,rd->...r', rows, proj, preferred_element_type=jnp.float32)  27.5 us
    gather x2, local copies, waits for them, and re-layouts, shards(): send_x = jnp.where(valid[:, None], tokens[tok], jnp.zeros((), tokens.dtype))  19.4 us
    all_to_all x1, starting transfers between devices, shards(): lax.all_to_all(xs_slots, 'expert', split_axis=0, concat_axis=0, tiled=True)  13.2 us
    gather x1, local copies, waits for them, and re-layouts, shards(): cotangent[tok].astype(jnp.float32)  11.8 us
  transfers between devices with their start and end apart: 3, of which 2 were waited for; matrix products, arithmetic and copies ran while one was open for 16% of the time, Pallas kernels for 0%

commit v1 on v0

v1 whole, which is shorter than its diff:
```python
import jax
import jax.numpy as jnp
from jax import lax
from jax.experimental import pallas as pl
from jax.experimental.pallas import tpu as pltpu
from jax.sharding import Mesh
from jax.sharding import PartitionSpec as P

NX, NZ, NC = 4, 8, 2
NJ = NX * NC
CAP, MAIN = 18, 16
SPARE = CAP - MAIN
EX_DEV = 2
BF, F32, I32 = jnp.bfloat16, jnp.float32, jnp.int32
VMEM = 60 * 1024 * 1024


def block_rows(n):
    return 2 * n * MAIN + 8


def row_slots(n, shard, array, offset_rows=0):
    r = lax.broadcasted_iota(I32, (block_rows(n), 1), 0)
    main = n * MAIN
    base = array * main + shard * MAIN
    spare = 2 * main + array * SPARE * n + shard * SPARE
    slot = jnp.where((r >= base) & (r < base + MAIN), r - base, -9)
    return jnp.where((r >= spare) & (r < spare + SPARE), MAIN + r - spare, slot)


def expert_keys(routes, ids):
    masks = [jnp.max(jnp.where(routes == e, 1.0, 0.0), axis=0, keepdims=True) for e in ids]
    mask = jnp.concatenate(masks, axis=0)
    t = mask.shape[1]
    before = lax.broadcasted_iota(I32, (t, t), 0) < lax.broadcasted_iota(I32, (t, t), 1)
    tri = jnp.where(before, 1.0, 0.0).astype(BF)
    rank = jnp.dot(mask.astype(BF), tri, preferred_element_type=F32)
    return jnp.where(mask > 0, rank, -1.0)


def dispatch(shard_refs, ids, tok_dev):
    n = len(shard_refs)
    rows = block_rows(n)
    d = shard_refs[0][0].shape[1]
    flat = [a for s in shard_refs for a in s]
    lens = [len(s) for s in shard_refs]

    def kernel(ids_ref, *refs):
        out_ref = refs[-1]
        eid = [ids_ref[j].astype(F32) for j in range(NJ)]
        acc, at = None, 0
        for a in range(n):
            shard = refs[at : at + lens[a]]
            at += lens[a]
            last = shard[-1]
            routes = last[last.shape[0] - 16 :, 0:tok_dev].astype(F32)[0:8]
            keys = expert_keys(routes, eid)
            parts = []
            for array in range(2):
                slots = row_slots(n, a, array).astype(F32)
                hot = [jnp.where(keys[j : j + 1] == slots, 1.0, 0.0) for j in range(NJ)]
                parts.append(jnp.concatenate(hot, axis=0))
            if len(shard) == 1:
                hot = jnp.concatenate(parts, axis=1).astype(BF)
                got = jnp.dot(hot, shard[0][0 : 2 * tok_dev, :], preferred_element_type=F32)
            else:
                got = jnp.dot(parts[0].astype(BF), shard[0][...], preferred_element_type=F32)
                got += jnp.dot(parts[1].astype(BF), shard[1][0:tok_dev, :], preferred_element_type=F32)
            acc = got if acc is None else acc + got
        for j in range(NJ):
            out_ref[j] = acc[j * rows : (j + 1) * rows].astype(BF)

    return pl.pallas_call(
        kernel,
        out_shape=jax.ShapeDtypeStruct((NJ, rows, d), BF),
        in_specs=[pl.BlockSpec(memory_space=pltpu.SMEM)] + [pl.BlockSpec(a.shape, lambda: (0, 0)) for a in flat],
        out_specs=pl.BlockSpec((NJ, rows, d), lambda: (0, 0, 0)),
        compiler_params=pltpu.CompilerParams(vmem_limit_bytes=VMEM),
    )(ids, *flat)


def expert(recv, n, w_gate, w_up, w_down, proj_in, proj_out):
    _, rows, d = recv.shape
    ff = w_gate.shape[1]
    r = proj_in.shape[0]
    chunk = 256
    main = n * MAIN
    m = NJ * main + NJ * 8
    contract = (((1,), (1,)), ((), ()))

    def kernel(x_ref, wg_ref, wu_ref, wd_ref, pi_ref, po_ref, out_ref, xs, cs, acc):
        f = pl.program_id(0)

        @pl.when(f == 0)
        def _():
            for j in range(NJ):
                xs[j * main : (j + 1) * main, :] = x_ref[j, 0:main, :]
                cs[j * main : (j + 1) * main, :] = x_ref[j, main : 2 * main, :]
            spare = [x_ref[j, 2 * main : 2 * main + 8, :].astype(F32) for j in range(NJ)]
            spare = jnp.concatenate(spare, axis=0).astype(BF)
            xs[NJ * main :, :] = spare
            cs[NJ * main :, :] = spare
            acc[...] = jnp.zeros_like(acc)

        x = xs[...]
        gate = jnp.dot(x, wg_ref[...], preferred_element_type=F32)
        up = jnp.dot(x, wu_ref[...], preferred_element_type=F32)
        back = lax.dot_general(cs[...], wd_ref[...], contract, preferred_element_type=F32)
        tail = back[NJ * main :]
        tail = jnp.concatenate([tail[2 * n :], tail[: 2 * n]], axis=0)
        back = jnp.concatenate([back[: NJ * main], tail], axis=0)
        sig = jax.nn.sigmoid(gate)
        hidden = (gate * sig * up).astype(BF)
        delta = (back * up * sig * (1.0 + gate * (1.0 - sig))).astype(BF)
        acc[:, 0:r] += lax.dot_general(hidden, pi_ref[...], contract, preferred_element_type=F32)
        acc[:, r:] += lax.dot_general(delta, po_ref[...], contract, preferred_element_type=F32)

        @pl.when(f == ff // chunk - 1)
        def _():
            for j in range(NJ):
                over = acc[NJ * main + 8 * j : NJ * main + 8 * j + 8]
                pieces = []
                for a in range(n):
                    lo = j * main + a * MAIN
                    pieces += [acc[lo : lo + MAIN], over]
                out_ref[j] = jnp.concatenate(pieces, axis=0).astype(BF)

    back_rows = n * (MAIN + 8)
    return pl.pallas_call(
        kernel,
        grid=(ff // chunk,),
        out_shape=jax.ShapeDtypeStruct((NJ, back_rows, 2 * r), BF),
        in_specs=[
            pl.BlockSpec((NJ, rows, d), lambda f: (0, 0, 0)),
            pl.BlockSpec((d, chunk), lambda f: (0, f)),
            pl.BlockSpec((d, chunk), lambda f: (0, f)),
            pl.BlockSpec((chunk, d), lambda f: (f, 0)),
            pl.BlockSpec((r, chunk), lambda f: (0, f)),
            pl.BlockSpec((r, chunk), lambda f: (0, f)),
        ],
        out_specs=pl.BlockSpec((NJ, back_rows, 2 * r), lambda f: (0, 0, 0)),
        scratch_shapes=[pltpu.VMEM((m, d), BF), pltpu.VMEM((m, d), BF), pltpu.VMEM((m, 2 * r), F32)],
        compiler_params=pltpu.CompilerParams(vmem_limit_bytes=VMEM),
    )(recv, w_gate, w_up, w_down, proj_in, proj_out)


def outer(ids, pieces, routes_t, weight_t, in_model, out_model, member):
    r = out_model.shape[1] // 2
    part = MAIN + 8
    k = NJ * part
    half = r // 2

    def kernel(ids_ref, routes_ref, weight_ref, im_ref, om_ref, mem_ref, *refs):
        out_ref = refs[-1]
        routes = routes_ref[...].astype(F32)
        weight = weight_ref[...]
        table = jnp.concatenate([im_ref[...], om_ref[...], mem_ref[...]], axis=1)
        lane = lax.broadcasted_iota(I32, (1, 2 * r), 1)
        col = lax.broadcasted_iota(I32, (k, NJ * 2 * r), 1) // (2 * r)
        row = lax.broadcasted_iota(I32, (k, NJ * 2 * r), 0) // part
        own = col == row
        pr = lax.broadcasted_iota(I32, (part, 1), 0)
        for p, (_, n, shard) in enumerate(pieces):
            eid = [ids_ref[p * NJ + j] for j in range(NJ)]
            keys = expert_keys(routes, [e.astype(F32) for e in eid])
            q = pr - MAIN - shard * SPARE
            slots = jnp.where(pr < MAIN, pr, jnp.where((q >= 0) & (q < SPARE), MAIN + q, -9)).astype(F32)
            hot, scale = [], []
            for j in range(NJ):
                h = jnp.where(keys[j : j + 1] == slots, 1.0, 0.0)
                we = jnp.sum(jnp.where(routes == eid[j].astype(F32), weight, 0.0), axis=0, keepdims=True)
                hot.append(h)
                scale.append(jnp.sum(h * we, axis=1, keepdims=True))
            hot = jnp.concatenate(hot, axis=0).astype(BF)
            scale = jnp.concatenate(scale, axis=0)
            sel = jnp.dot(hot, table, preferred_element_type=F32)
            im = sel[:, 0 : 2 * r] * scale
            om = sel[:, 2 * r : 4 * r] * scale
            mem = sel[:, 4 * r : 6 * r]
            ret = refs[p]
            got = [ret[j, shard * part : (shard + 1) * part, :].astype(F32) for j in range(NJ)]
            got = jnp.concatenate(got, axis=0)
            inner = jnp.concatenate([got[:, 0:r], got[:, 0:r]], axis=1) * mem
            outh = jnp.concatenate([got[:, r:], got[:, r:]], axis=1)
            for g, (left, right) in enumerate(((im, outh), (inner, om))):
                wide = jnp.concatenate([right] * NJ, axis=1)
                wide = jnp.where(own, wide, 0.0).astype(BF)
                res = lax.dot_general(
                    left.astype(BF), wide, (((0,), (0,)), ((), ())), preferred_element_type=F32
                )
                for j in range(NJ):
                    for s in range(EX_DEV):
                        even = res[s * r : s * r + half, j * 2 * r : (j + 1) * 2 * r]
                        odd = res[s * r + half : (s + 1) * r, j * 2 * r : (j + 1) * 2 * r]
                        out_ref[s, eid[j], g] = jnp.where(lane < r, even, odd).astype(BF)

    arrays = [a for a, _, _ in pieces]
    vmem = pl.BlockSpec(memory_space=pltpu.VMEM)
    return pl.pallas_call(
        kernel,
        out_shape=jax.ShapeDtypeStruct((EX_DEV, NZ * NJ, 2, half, 2 * r), BF),
        in_specs=[pl.BlockSpec(memory_space=pltpu.SMEM)] + [vmem] * (5 + len(arrays)),
        out_specs=vmem,
        compiler_params=pltpu.CompilerParams(vmem_limit_bytes=VMEM),
    )(ids, routes_t, weight_t, in_model, out_model, member, *arrays)


def along_z(a, k):
    return lax.ppermute(a, "z", [(i, (i + k) % NZ) for i in range(NZ)])


def plane_exchange(a):
    return lax.all_to_all(a, ("x", "c"), split_axis=0, concat_axis=0, tiled=True)


def shards(
    tokens, cotangent, routes, route_weight, example_ids, w_gate, w_up, w_down, proj_model, proj_hidden
):
    tok_dev, d = tokens.shape
    r = proj_model.shape[0]
    z = lax.axis_index("z")
    j = jnp.arange(NJ, dtype=I32)
    plane = lambda zz: (j // NC) * (NZ * NC) + zz * NC + j % NC
    here = plane(z)

    routes_t = routes.T
    weight_t = route_weight.T
    extra = jnp.pad(routes_t.astype(BF), ((0, 8), (0, d - tok_dev)))
    own = jnp.concatenate([tokens, cotangent, extra], axis=0)
    split = tok_dev

    order = lambda p: jnp.concatenate([p[0::2], p[1::2]], axis=0)
    proj_in, proj_out = order(proj_hidden), proj_hidden
    wg, wu, wd = w_gate[0], w_up[0], w_down[0]

    fwd = back = own
    shard_steps = [([(own,)], [0])]
    for s in (1, 2, 3):
        fwd, back = along_z(fwd, 1), along_z(back, -1)
        shard_steps.append(([(fwd,), (back,)], [-s, s]))
    top, bottom = along_z(fwd[:split], 1), along_z(back[split:], -1)
    shard_steps.append(([(top, bottom)], [4]))

    pieces, ids = [], []
    for refs, dist in shard_steps:
        n = len(refs)
        got = plane_exchange(dispatch(refs, here, tok_dev))
        ret = plane_exchange(expert(got, n, wg, wu, wd, proj_in, proj_out))
        for a, k in enumerate(dist):
            pieces.append((ret if k == 0 else along_z(ret, k), n, a))
            ids.append(plane((z - k) % NZ))

    dot = lambda a, p: lax.dot_general(a, p, (((1,), (1,)), ((), ())), preferred_element_type=F32)
    in_model = dot(tokens, order(proj_model)).astype(BF)
    out_model = dot(cotangent, proj_model).astype(BF)
    lanes = jnp.arange(2 * r, dtype=I32)[None, :] // r
    member = (example_ids[:, None] == lanes).astype(BF)
    in_model = jnp.concatenate([in_model, in_model], axis=1) * member
    out_model = jnp.concatenate([out_model, out_model], axis=1)
    out = outer(jnp.concatenate(ids), pieces, routes_t, weight_t, in_model, out_model, member)
    return out.reshape(EX_DEV, NZ * NJ, 2, r * r)


def solution(mesh):
    dp = mesh.shape["dp"]
    torus = Mesh(mesh.devices.reshape(dp, NX, NZ, NC), ("dp", "x", "z", "c"))
    part, ex = ("dp", "x", "z", "c"), ("x", "z", "c")
    placed = (
        P(part, None),
        P(part, None),
        P(part, None),
        P(part, None),
        P(part),
        P(ex, None, None),
        P(ex, None, None),
        P(ex, None, None),
        P(),
        P(),
    )
    return jax.shard_map(
        shards, mesh=torus, in_specs=placed, out_specs=P(part, None, None, None), check_vma=False
    )
```

time: 509 us -> 284 us (0.56); the launches traced: 499 us -> 282 us
  waiting for transfers between devices: 225 us -> 114 us
  local copies, waits for them, and re-layouts: 94.6 us -> 15.1 us
  Pallas kernels: 0 us -> 68.5 us
  blocking collectives: 61.4 us -> 0 us
  starting transfers between devices: 25.9 us -> 76.7 us
  other arithmetic: 48.9 us -> 5.67 us
  matrix products: 42.4 us -> 1.64 us
    all_to_all x3 -> x10, waiting for transfers between devices: 225 us -> 31.7 us  [plane_exchange(): lax.all_to_all(a, ('x', 'c'), split_axis=0, concat_axis=0, tiled=True)]
    ppermute x0 -> x15, waiting for transfers between devices: none -> 82.5 us  [along_z(): return lax.ppermute(a, 'z', [(i, (i + k) % NZ) for i in range(NZ)])]
    pallas_call x0 -> x11, Pallas kernels: none -> 68.5 us  [the longest x5 41.8 us: expert(): pl.pallas_call(kernel, grid=(ff // chunk,), out_shape=jax.ShapeDtypeStruc...]
    all_to_all x1 -> x0, blocking collectives: 61.4 us -> none  [shards(): lax.all_to_all(blocks, 'expert', split_axis=1, concat_axis=1, tiled=True)]
    gather x5 -> x0, local copies, waits for them, and re-layouts: 42.7 us -> none  [the longest x2 19.4 us: shards(): send_x = jnp.where(valid[:, None], tokens[tok], jnp.zeros((), tokens.dtype))]
    dot_general x8 -> x2, matrix products: 42.4 us -> 1.64 us  [shards(): lax.dot_general(a, p, (((1,), (1,)), ((), ())), preferred_element_type=F32)]
    another operation x4 -> x0, other arithmetic: 32.7 us -> none
    all_to_all x3 -> x10, starting transfers between devices: 25.9 us -> 51.3 us  [plane_exchange(): lax.all_to_all(a, ('x', 'c'), split_axis=0, concat_axis=0, tiled=True)]
  transfers between devices with their start and end apart: 3 -> 25, of which waited for: 2 -> 9; matrix products, arithmetic and copies ran while one was open for 16% -> 2% of each run, Pallas kernels for 0% -> 21%
where the time goes in v1:
time: 284 us; the launch traced here: 282 us
  waiting for transfers between devices  114 us (40%)
  starting transfers between devices  76.7 us (27%)
  Pallas kernels  68.5 us (24%)
  local copies, waits for them, and re-layouts  15.1 us (5%)
  other arithmetic  5.67 us (2%)
    ppermute x15, waiting for transfers between devices, along_z(): return lax.ppermute(a, 'z', [(i, (i + k) % NZ) for i in range(NZ)])  82.5 us
    all_to_all x10, starting transfers between devices, plane_exchange(): lax.all_to_all(a, ('x', 'c'), split_axis=0, concat_axis=0, tiled=True)  51.3 us
    pallas_call x5, Pallas kernels, expert(): pl.pallas_call(kernel, grid=(ff // chunk,), out_shape=jax.ShapeDtypeStruc...  41.8 us
    all_to_all x10, waiting for transfers between devices, plane_exchange(): lax.all_to_all(a, ('x', 'c'), split_axis=0, concat_axis=0, tiled=True)  31.7 us
    ppermute x15, starting transfers between devices, along_z(): return lax.ppermute(a, 'z', [(i, (i + k) % NZ) for i in range(NZ)])  25.4 us
    pallas_call x5, Pallas kernels, dispatch(): pl.pallas_call(kernel, out_shape=jax.ShapeDtypeStruct((NJ, rows, d), BF),...  19.9 us
    unnamed x50, local copies, waits for them, and re-layouts  9.77 us
    pallas_call x1, Pallas kernels, outer(): pl.pallas_call(kernel, out_shape=jax.ShapeDtypeStruct((EX_DEV, NZ * NJ, 2...  6.81 us
  transfers between devices with their start and end apart: 25, of which 9 were waited for; matrix products, arithmetic and copies ran while one was open for 2% of the time, Pallas kernels for 21%

profile of v1, /device:TPU:1, one launch (start us, length us, event | category | flops | bytes accessed | tf_op | source)
XLA Modules:
  0.0 282.1 jit_solution(17719623915719231505)
XLA Ops:
  6.6 6.7 %all-to-all-start = ((bf16[8,40,2048]{2,1,0:T(8,128)(2,1)}), bf16[8,40,2048]{2,1,0:T(8,128)(2,1)S(1)}, u32[]{:S(2)}, u32[]{:S(2)}) async-start(bf16[8,40,2048]{2,1,0:T(8,128)(2,1)} %shard_map.100), calls=%async_computation | async-start | bytes 2621440 | tf_op jit(solution)/shard_map/all_to_all | solution.py:213
  18.1 24.8 %collective-permute-done.refs_0_ = bf16[272,2048]{1,0:T(8,128)(2,1)S(1)} collective-permute-done((bf16[272,2048]{1,0:T(8,128)(2,1)S(1)}, bf16[272,2048]{1,0:T(8,128)(2,1)S(1)}, u32[]{:S(2)}, u32[]{:S(2)}) %collective-permute-start) | collective-permute-done | bytes 1114144 | tf_op jit(solution)/shard_map/ppermute | solution.py:209
  43.8 4.6 %shard_map.102 = bf16[8,72,2048]{2,1,0:T(8,128)(2,1)} custom-call(s32[8]{0:T(128)} %add_add_fusion.ids_ref, bf16[272,2048]{1,0:T(8,128)(2,1)} %copy-done.10, bf16[272,2048]{1,0:T(8,128)(2,1)} %collective-permute-done.1.refs_1_), custom_call_target="tpu_custom_call" | custom-call | tf_op jit(solution)/shard_map/pallas_call | solution.py:73
  49.5 5.1 %all-to-all-start.2 = ((bf16[8,72,2048]{2,1,0:T(8,128)(2,1)}), bf16[8,72,2048]{2,1,0:T(8,128)(2,1)S(1)}, u32[]{:S(2)}, u32[]{:S(2)}) async-start(bf16[8,72,2048]{2,1,0:T(8,128)(2,1)} %shard_map.102), calls=%async_computation.2 | async-start | bytes 4718592 | tf_op jit(solution)/shard_map/all_to_all | solution.py:213
  57.2 24.9 %collective-permute-done.4.refs_0_ = bf16[272,2048]{1,0:T(8,128)(2,1)S(1)} collective-permute-done((bf16[272,2048]{1,0:T(8,128)(2,1)}, bf16[272,2048]{1,0:T(8,128)(2,1)S(1)}, u32[]{:S(2)}, u32[]{:S(2)}) %collective-permute-start.4) | collective-permute-done | bytes 1114144 | tf_op jit(solution)/shard_map/ppermute | solution.py:209
  83.2 4.5 %shard_map.104 = bf16[8,72,2048]{2,1,0:T(8,128)(2,1)} custom-call(s32[8]{0:T(128)} %add_add_fusion.ids_ref, bf16[272,2048]{1,0:T(8,128)(2,1)} %copy-done.9, bf16[272,2048]{1,0:T(8,128)(2,1)} %collective-permute-done.5.refs_1_), custom_call_target="tpu_custom_call" | custom-call | tf_op jit(solution)/shard_map/pallas_call | solution.py:73
  89.1 5.2 %all-to-all-start.4 = ((bf16[8,72,2048]{2,1,0:T(8,128)(2,1)}), bf16[8,72,2048]{2,1,0:T(8,128)(2,1)}, u32[]{:S(2)}, u32[]{:S(2)}) async-start(bf16[8,72,2048]{2,1,0:T(8,128)(2,1)} %shard_map.104), calls=%async_computation.4 | async-start | bytes 4718592 | tf_op jit(solution)/shard_map/all_to_all | solution.py:213
  96.1 24.6 %collective-permute-done.9.refs_1_ = bf16[272,2048]{1,0:T(8,128)(2,1)S(1)} collective-permute-done((bf16[272,2048]{1,0:T(8,128)(2,1)}, bf16[272,2048]{1,0:T(8,128)(2,1)S(1)}, u32[]{:S(2)}, u32[]{:S(2)}) %collective-permute-start.9) | collective-permute-done | bytes 1114144 | tf_op jit(solution)/shard_map/ppermute | solution.py:209
  126.8 8.8 %shard_map.103 = bf16[8,48,128]{2,1,0:T(8,128)(2,1)} custom-call(bf16[8,72,2048]{2,1,0:T(8,128)(2,1)} %copy-done.1, bf16[2048,768]{1,0:T(8,128)(2,1)} %bitcast.12, bf16[2048,768]{1,0:T(8,128)(2,1)} %bitcast.17, bf16[768,2048]{1,0:T(8,128)(2,1)} %bitcast.22, bf16[64,768]{1,0:T(8,128)(2,1)} %pad_maximum_fusion.pi_ref, bf16[64,768]{1,0:T(8,128)(2,1)} %po_ref.9), custom_call_target="tpu_custom_call" | custom-call | tf_op jit(solution)/shard_map/pallas_call | solution.py:129
  135.6 5.5 %all-to-all-start.3 = ((bf16[8,48,128]{2,1,0:T(8,128)(2,1)}), bf16[8,48,128]{2,1,0:T(8,128)(2,1)S(1)}, u32[]{:S(2)}, u32[]{:S(2)}) async-start(bf16[8,48,128]{2,1,0:T(8,128)(2,1)} %shard_map.103), calls=%async_computation.3 | async-start | bytes 196608 | tf_op jit(solution)/shard_map/all_to_all | solution.py:213
  141.0 8.8 %shard_map.105 = bf16[8,48,128]{2,1,0:T(8,128)(2,1)} custom-call(bf16[8,72,2048]{2,1,0:T(8,128)(2,1)} %all-to-all-done.4.x_ref, bf16[2048,768]{1,0:T(8,128)(2,1)} %bitcast.13, bf16[2048,768]{1,0:T(8,128)(2,1)} %bitcast.18, bf16[768,2048]{1,0:T(8,128)(2,1)} %bitcast.23, bf16[64,768]{1,0:T(8,128)(2,1)} %pad_maximum_fusion.pi_ref, bf16[64,768]{1,0:T(8,128)(2,1)} %po_ref.9), custom_call_target="tpu_custom_call" | custom-call | tf_op jit(solution)/shard_map/pallas_call | solution.py:129
  149.8 4.8 %all-to-all-start.5 = ((bf16[8,48,128]{2,1,0:T(8,128)(2,1)}), bf16[8,48,128]{2,1,0:T(8,128)(2,1)S(1)}, u32[]{:S(2)}, u32[]{:S(2)}) async-start(bf16[8,48,128]{2,1,0:T(8,128)(2,1)} %shard_map.105), calls=%async_computation.5 | async-start | bytes 196608 | tf_op jit(solution)/shard_map/all_to_all | solution.py:213
  159.6 4.7 %all-to-all-start.8 = ((bf16[8,40,2048]{2,1,0:T(8,128)(2,1)}), bf16[8,40,2048]{2,1,0:T(8,128)(2,1)S(1)}, u32[]{:S(2)}, u32[]{:S(2)}) async-start(bf16[8,40,2048]{2,1,0:T(8,128)(2,1)} %shard_map.108), calls=%async_computation.8 | async-start | bytes 2621440 | tf_op jit(solution)/shard_map/all_to_all | solution.py:213
  164.3 4.5 %shard_map.106 = bf16[8,72,2048]{2,1,0:T(8,128)(2,1)} custom-call(s32[8]{0:T(128)} %add_add_fusion.ids_ref, bf16[272,2048]{1,0:T(8,128)(2,1)} %copy-done.7, bf16[272,2048]{1,0:T(8,128)(2,1)} %copy-done.6), custom_call_target="tpu_custom_call" | custom-call | tf_op jit(solution)/shard_map/pallas_call | solution.py:73
  168.9 13.4 %all-to-all-done.8.x_ref = bf16[8,40,2048]{2,1,0:T(8,128)(2,1)S(1)} async-done(((bf16[8,40,2048]{2,1,0:T(8,128)(2,1)}), bf16[8,40,2048]{2,1,0:T(8,128)(2,1)S(1)}, u32[]{:S(2)}, u32[]{:S(2)}) %all-to-all-start.8) | async-done | bytes 1310752 | tf_op jit(solution)/shard_map/all_to_all | solution.py:213
  183.3 4.4 %all-to-all-start.6 = ((bf16[8,72,2048]{2,1,0:T(8,128)(2,1)}), bf16[8,72,2048]{2,1,0:T(8,128)(2,1)S(1)}, u32[]{:S(2)}, u32[]{:S(2)}) async-start(bf16[8,72,2048]{2,1,0:T(8,128)(2,1)} %shard_map.106), calls=%async_computation.6 | async-start | bytes 4718592 | tf_op jit(solution)/shard_map/all_to_all | solution.py:213
  191.4 7.7 %shard_map.109 = bf16[8,24,128]{2,1,0:T(8,128)(2,1)} custom-call(bf16[8,40,2048]{2,1,0:T(8,128)(2,1)} %copy-done.3, bf16[2048,768]{1,0:T(8,128)(2,1)} %bitcast.14, bf16[2048,768]{1,0:T(8,128)(2,1)} %bitcast.19, bf16[768,2048]{1,0:T(8,128)(2,1)} %bitcast.24, bf16[64,768]{1,0:T(8,128)(2,1)} %pad_maximum_fusion.pi_ref, bf16[64,768]{1,0:T(8,128)(2,1)} %po_ref.9), custom_call_target="tpu_custom_call" | custom-call | tf_op jit(solution)/shard_map/pallas_call | solution.py:129
  199.2 17.7 %all-to-all-done.6.x_ref = bf16[8,72,2048]{2,1,0:T(8,128)(2,1)S(1)} async-done(((bf16[8,72,2048]{2,1,0:T(8,128)(2,1)}), bf16[8,72,2048]{2,1,0:T(8,128)(2,1)S(1)}, u32[]{:S(2)}, u32[]{:S(2)}) %all-to-all-start.6) | async-done | bytes 2359328 | tf_op jit(solution)/shard_map/all_to_all | solution.py:213
  224.0 8.8 %shard_map.107 = bf16[8,48,128]{2,1,0:T(8,128)(2,1)} custom-call(bf16[8,72,2048]{2,1,0:T(8,128)(2,1)} %copy-done, bf16[2048,768]{1,0:T(8,128)(2,1)} %bitcast.15, bf16[2048,768]{1,0:T(8,128)(2,1)} %bitcast.20, bf16[768,2048]{1,0:T(8,128)(2,1)} %bitcast.25, bf16[64,768]{1,0:T(8,128)(2,1)} %pad_maximum_fusion.pi_ref, bf16[64,768]{1,0:T(8,128)(2,1)} %po_ref.9), custom_call_target="tpu_custom_call" | custom-call | tf_op jit(solution)/shard_map/pallas_call | solution.py:129
  232.8 5.1 %all-to-all-start.7 = ((bf16[8,48,128]{2,1,0:T(8,128)(2,1)}), bf16[8,48,128]{2,1,0:T(8,128)(2,1)S(1)}, u32[]{:S(2)}, u32[]{:S(2)}) async-start(bf16[8,48,128]{2,1,0:T(8,128)(2,1)} %shard_map.107), calls=%async_computation.7 | async-start | bytes 196608 | tf_op jit(solution)/shard_map/all_to_all | solution.py:213
  237.9 7.7 %shard_map.101 = bf16[8,24,128]{2,1,0:T(8,128)(2,1)} custom-call(bf16[8,40,2048]{2,1,0:T(8,128)(2,1)} %copy-done.2, bf16[2048,768]{1,0:T(8,128)(2,1)} %bitcast.16, bf16[2048,768]{1,0:T(8,128)(2,1)} %bitcast.21, bf16[768,2048]{1,0:T(8,128)(2,1)} %bitcast.26, bf16[64,768]{1,0:T(8,128)(2,1)} %pad_maximum_fusion.pi_ref, bf16[64,768]{1,0:T(8,128)(2,1)} %po_ref.9), custom_call_target="tpu_custom_call" | custom-call | tf_op jit(solution)/shard_map/pallas_call | solution.py:129
  252.0 5.6 %all-to-all-start.1 = ((bf16[8,24,128]{2,1,0:T(8,128)(2,1)}), bf16[8,24,128]{2,1,0:T(8,128)(2,1)S(1)}, u32[]{:S(2)}, u32[]{:S(2)}) async-start(bf16[8,24,128]{2,1,0:T(8,128)(2,1)} %shard_map.101), calls=%async_computation.1 | async-start | bytes 98304 | tf_op jit(solution)/shard_map/all_to_all | solution.py:213
  262.5 5.9 %collective-permute-done.10.refs_5_ = bf16[8,48,128]{2,1,0:T(8,128)(2,1)S(1)} collective-permute-done((bf16[8,48,128]{2,1,0:T(8,128)(2,1)S(1)}, bf16[8,48,128]{2,1,0:T(8,128)(2,1)S(1)}, u32[]{:S(2)}, u32[]{:S(2)}) %collective-permute-start.10) | collective-permute-done | bytes 98336 | tf_op jit(solution)/shard_map/ppermute | solution.py:209
  271.3 6.8 %shard_map.110 = bf16[2,64,2,32,128]{4,3,2,1,0:T(8,128)(2,1)} custom-call(s32[64]{0:T(128)} %concatenate.18.ids_ref, s32[8,128]{1,0:T(8,128)} %bitcast.28, f32[8,128]{1,0:T(8,128)} %bitcast.29, bf16[128,128]{1,0:T(8,128)(2,1)} %get-tuple-element.13.im_ref, bf16[128,128]{1,0:T(8,128)(2,1)} %get-tuple-element.14.om_ref, ...), custom_call_target="tpu_custom_call" | custom-call | tf_op jit(solution)/shard_map/pallas_call | solution.py:199
  (110 shorter events, 61.1 us)
Async XLA Ops:
  6.6 41.8 %all-to-all-start = ((bf16[8,40,2048]{2,1,0:T(8,128)(2,1)}), bf16[8,40,2048]{2,1,0:T(8,128)(2,1)S(1)}, u32[]{:S(2)}, u32[]{:S(2)}) async-start(bf16[8,40,2048]{2,1,0:T(8,128)(2,1)} %shard_map.100), calls=%async_computation | async-start | bytes 2621440 | tf_op jit(solution)/shard_map/all_to_all | solution.py:213
  13.3 29.5 %collective-permute-start = (bf16[272,2048]{1,0:T(8,128)(2,1)S(1)}, bf16[272,2048]{1,0:T(8,128)(2,1)S(1)}, u32[]{:S(2)}, u32[]{:S(2)}) collective-permute-start(bf16[272,2048]{1,0:T(8,128)(2,1)S(1)} %copy-done.4), channel_id=1, source_target_pairs={{0,2},{2,4},{4,6},{6,8},{8,10},{10,12},{12,14},{14,0},{1,3},{3,5},... | collective-permute-start | bytes 3342344 | tf_op jit(solution)/shard_map/ppermute | solution.py:209
  14.0 28.8 %collective-permute-start.1 = (bf16[272,2048]{1,0:T(8,128)(2,1)S(1)}, bf16[272,2048]{1,0:T(8,128)(2,1)}, u32[]{:S(2)}, u32[]{:S(2)}) collective-permute-start(bf16[272,2048]{1,0:T(8,128)(2,1)S(1)} %copy-done.4), channel_id=1, source_target_pairs={{0,14},{2,0},{4,2},{6,4},{8,6},{10,8},{12,10},{14,12},{1,15},{3,1}... | collective-permute-start | bytes 3342344 | tf_op jit(solution)/shard_map/ppermute | solution.py:209
  49.5 38.2 %all-to-all-start.2 = ((bf16[8,72,2048]{2,1,0:T(8,128)(2,1)}), bf16[8,72,2048]{2,1,0:T(8,128)(2,1)S(1)}, u32[]{:S(2)}, u32[]{:S(2)}) async-start(bf16[8,72,2048]{2,1,0:T(8,128)(2,1)} %shard_map.102), calls=%async_computation.2 | async-start | bytes 4718592 | tf_op jit(solution)/shard_map/all_to_all | solution.py:213
  54.6 27.6 %collective-permute-start.4 = (bf16[272,2048]{1,0:T(8,128)(2,1)}, bf16[272,2048]{1,0:T(8,128)(2,1)S(1)}, u32[]{:S(2)}, u32[]{:S(2)}) collective-permute-start(bf16[272,2048]{1,0:T(8,128)(2,1)} %copy-done.10), channel_id=1, source_target_pairs={{0,2},{2,4},{4,6},{6,8},{8,10},{10,12},{12,14},{14,0},{1,3},{3,5},... | collective-permute-start | bytes 3342344 | tf_op jit(solution)/shard_map/ppermute | solution.py:209
  54.6 27.6 %collective-permute-start.5 = (bf16[272,2048]{1,0:T(8,128)(2,1)}, bf16[272,2048]{1,0:T(8,128)(2,1)}, u32[]{:S(2)}, u32[]{:S(2)}) collective-permute-start(bf16[272,2048]{1,0:T(8,128)(2,1)} %collective-permute-done.1.refs_1_), channel_id=1, source_target_pairs={{0,14},{2,0},{4,2},{6,4},{8,6},{10,8},{12,10},{14,12},{1,15},{3,1}... | collective-permute-start | bytes 3342344 | tf_op jit(solution)/shard_map/ppermute | solution.py:209
  89.1 46.5 %all-to-all-start.4 = ((bf16[8,72,2048]{2,1,0:T(8,128)(2,1)}), bf16[8,72,2048]{2,1,0:T(8,128)(2,1)}, u32[]{:S(2)}, u32[]{:S(2)}) async-start(bf16[8,72,2048]{2,1,0:T(8,128)(2,1)} %shard_map.104), calls=%async_computation.4 | async-start | bytes 4718592 | tf_op jit(solution)/shard_map/all_to_all | solution.py:213
  94.3 26.4 %collective-permute-start.9 = (bf16[272,2048]{1,0:T(8,128)(2,1)}, bf16[272,2048]{1,0:T(8,128)(2,1)S(1)}, u32[]{:S(2)}, u32[]{:S(2)}) collective-permute-start(bf16[272,2048]{1,0:T(8,128)(2,1)} %collective-permute-done.5.refs_1_), channel_id=1, source_target_pairs={{0,14},{2,0},{4,2},{6,4},{8,6},{10,8},{12,10},{14,12},{1,15},{3,1}... | collective-permute-start | bytes 3342344 | tf_op jit(solution)/shard_map/ppermute | solution.py:209
  96.1 28.8 %collective-permute-start.8 = (bf16[272,2048]{1,0:T(8,128)(2,1)}, bf16[272,2048]{1,0:T(8,128)(2,1)S(1)}, u32[]{:S(2)}, u32[]{:S(2)}) collective-permute-start(bf16[272,2048]{1,0:T(8,128)(2,1)} %copy-done.9), channel_id=1, source_target_pairs={{0,2},{2,4},{4,6},{6,8},{8,10},{10,12},{12,14},{14,0},{1,3},{3,5},... | collective-permute-start | bytes 3342344 | tf_op jit(solution)/shard_map/ppermute | solution.py:209
  121.8 32.8 %collective-permute-start.13 = (bf16[144,2048]{1,0:T(8,128)(2,1)S(1)}, bf16[144,2048]{1,0:T(8,128)(2,1)S(1)}, u32[]{:S(2)}, u32[]{:S(2)}) collective-permute-start(bf16[144,2048]{1,0:T(8,128)(2,1)S(1)} %slice.25), channel_id=1, source_target_pairs={{0,14},{2,0},{4,2},{6,4},{8,6},{10,8},{12,10},{14,12},{1,15},{3,1}... | collective-permute-start | bytes 1769480 | tf_op jit(solution)/shard_map/ppermute | solution.py:209
  126.0 28.7 %collective-permute-start.12 = (bf16[128,2048]{1,0:T(8,128)(2,1)S(1)}, bf16[128,2048]{1,0:T(8,128)(2,1)S(1)}, u32[]{:S(2)}, u32[]{:S(2)}) collective-permute-start(bf16[128,2048]{1,0:T(8,128)(2,1)S(1)} %slice.24), channel_id=1, source_target_pairs={{0,2},{2,4},{4,6},{6,8},{8,10},{10,12},{12,14},{14,0},{1,3},{3,5},... | collective-permute-start | bytes 1572872 | tf_op jit(solution)/shard_map/ppermute | solution.py:209
  135.6 14.2 %all-to-all-start.3 = ((bf16[8,48,128]{2,1,0:T(8,128)(2,1)}), bf16[8,48,128]{2,1,0:T(8,128)(2,1)S(1)}, u32[]{:S(2)}, u32[]{:S(2)}) async-start(bf16[8,48,128]{2,1,0:T(8,128)(2,1)} %shard_map.103), calls=%async_computation.3 | async-start | bytes 196608 | tf_op jit(solution)/shard_map/all_to_all | solution.py:213
  159.6 22.6 %all-to-all-start.8 = ((bf16[8,40,2048]{2,1,0:T(8,128)(2,1)}), bf16[8,40,2048]{2,1,0:T(8,128)(2,1)S(1)}, u32[]{:S(2)}, u32[]{:S(2)}) async-start(bf16[8,40,2048]{2,1,0:T(8,128)(2,1)} %shard_map.108), calls=%async_computation.8 | async-start | bytes 2621440 | tf_op jit(solution)/shard_map/all_to_all | solution.py:213
  183.3 33.6 %all-to-all-start.6 = ((bf16[8,72,2048]{2,1,0:T(8,128)(2,1)}), bf16[8,72,2048]{2,1,0:T(8,128)(2,1)S(1)}, u32[]{:S(2)}, u32[]{:S(2)}) async-start(bf16[8,72,2048]{2,1,0:T(8,128)(2,1)} %shard_map.106), calls=%async_computation.6 | async-start | bytes 4718592 | tf_op jit(solution)/shard_map/all_to_all | solution.py:213
  216.9 15.9 %all-to-all-start.9 = ((bf16[8,24,128]{2,1,0:T(8,128)(2,1)}), bf16[8,24,128]{2,1,0:T(8,128)(2,1)S(1)}, u32[]{:S(2)}, u32[]{:S(2)}) async-start(bf16[8,24,128]{2,1,0:T(8,128)(2,1)} %shard_map.109), calls=%async_computation.9 | async-start | bytes 98304 | tf_op jit(solution)/shard_map/all_to_all | solution.py:213
  221.0 36.7 %collective-permute-start.2 = (bf16[8,48,128]{2,1,0:T(8,128)(2,1)S(1)}, bf16[8,48,128]{2,1,0:T(8,128)(2,1)S(1)}, u32[]{:S(2)}, u32[]{:S(2)}) collective-permute-start(bf16[8,48,128]{2,1,0:T(8,128)(2,1)S(1)} %copy-done.22), channel_id=1, source_target_pairs={{0,14},{2,0},{4,2},{6,4},{8,6},{10,8},{12,10},{14,12},{1,15},{3,1}... | collective-permute-start | bytes 294920 | tf_op jit(solution)/shard_map/ppermute | solution.py:209
  224.0 36.3 %collective-permute-start.3 = (bf16[8,48,128]{2,1,0:T(8,128)(2,1)S(1)}, bf16[8,48,128]{2,1,0:T(8,128)(2,1)S(1)}, u32[]{:S(2)}, u32[]{:S(2)}) collective-permute-start(bf16[8,48,128]{2,1,0:T(8,128)(2,1)S(1)} %copy-done.22), channel_id=1, source_target_pairs={{0,2},{2,4},{4,6},{6,8},{8,10},{10,12},{12,14},{14,0},{1,3},{3,5},... | collective-permute-start | bytes 294920 | tf_op jit(solution)/shard_map/ppermute | solution.py:209
  232.8 19.2 %all-to-all-start.7 = ((bf16[8,48,128]{2,1,0:T(8,128)(2,1)}), bf16[8,48,128]{2,1,0:T(8,128)(2,1)S(1)}, u32[]{:S(2)}, u32[]{:S(2)}) async-start(bf16[8,48,128]{2,1,0:T(8,128)(2,1)} %shard_map.107), calls=%async_computation.7 | async-start | bytes 196608 | tf_op jit(solution)/shard_map/all_to_all | solution.py:213
  245.6 16.8 %collective-permute-start.6 = (bf16[8,48,128]{2,1,0:T(8,128)(2,1)S(1)}, bf16[8,48,128]{2,1,0:T(8,128)(2,1)S(1)}, u32[]{:S(2)}, u32[]{:S(2)}) collective-permute-start(bf16[8,48,128]{2,1,0:T(8,128)(2,1)S(1)} %all-to-all-done.5), channel_id=1, source_target_pairs={{0,12},{2,14},{4,0},{6,2},{8,4},{10,6},{12,8},{14,10},{1,13},{3,15... | collective-permute-start | bytes 294920 | tf_op jit(solution)/shard_map/ppermute | solution.py:209
  246.9 15.6 %collective-permute-start.7 = (bf16[8,48,128]{2,1,0:T(8,128)(2,1)S(1)}, bf16[8,48,128]{2,1,0:T(8,128)(2,1)S(1)}, u32[]{:S(2)}, u32[]{:S(2)}) collective-permute-start(bf16[8,48,128]{2,1,0:T(8,128)(2,1)S(1)} %all-to-all-done.5), channel_id=1, source_target_pairs={{0,4},{2,6},{4,8},{6,10},{8,12},{10,14},{12,0},{14,2},{1,5},{3,7},... | collective-permute-start | bytes 294920 | tf_op jit(solution)/shard_map/ppermute | solution.py:209
  248.0 14.5 %collective-permute-start.14 = (bf16[8,24,128]{2,1,0:T(8,128)(2,1)S(1)}, bf16[8,24,128]{2,1,0:T(8,128)(2,1)S(1)}, u32[]{:S(2)}, u32[]{:S(2)}) collective-permute-start(bf16[8,24,128]{2,1,0:T(8,128)(2,1)S(1)} %all-to-all-done.9), channel_id=1, source_target_pairs={{0,8},{2,10},{4,12},{6,14},{8,0},{10,2},{12,4},{14,6},{1,9},{3,11}... | collective-permute-start | bytes 147464 | tf_op jit(solution)/shard_map/ppermute | solution.py:209
  252.0 10.4 %all-to-all-start.1 = ((bf16[8,24,128]{2,1,0:T(8,128)(2,1)}), bf16[8,24,128]{2,1,0:T(8,128)(2,1)S(1)}, u32[]{:S(2)}, u32[]{:S(2)}) async-start(bf16[8,24,128]{2,1,0:T(8,128)(2,1)} %shard_map.101), calls=%async_computation.1 | async-start | bytes 98304 | tf_op jit(solution)/shard_map/all_to_all | solution.py:213
  257.7 10.8 %collective-permute-start.10 = (bf16[8,48,128]{2,1,0:T(8,128)(2,1)S(1)}, bf16[8,48,128]{2,1,0:T(8,128)(2,1)S(1)}, u32[]{:S(2)}, u32[]{:S(2)}) collective-permute-start(bf16[8,48,128]{2,1,0:T(8,128)(2,1)S(1)} %all-to-all-done.7), channel_id=1, source_target_pairs={{0,10},{2,12},{4,14},{6,0},{8,2},{10,4},{12,6},{14,8},{1,11},{3,13... | collective-permute-start | bytes 294920 | tf_op jit(solution)/shard_map/ppermute | solution.py:209
  260.3 10.3 %collective-permute-start.11 = (bf16[8,48,128]{2,1,0:T(8,128)(2,1)S(1)}, bf16[8,48,128]{2,1,0:T(8,128)(2,1)S(1)}, u32[]{:S(2)}, u32[]{:S(2)}) collective-permute-start(bf16[8,48,128]{2,1,0:T(8,128)(2,1)S(1)} %all-to-all-done.7), channel_id=1, source_target_pairs={{0,6},{2,8},{4,10},{6,12},{8,14},{10,0},{12,2},{14,4},{1,7},{3,9},... | collective-permute-start | bytes 294920 | tf_op jit(solution)/shard_map/ppermute | solution.py:209
  (26 other events, 208.1 us)

commit v2 on v1

--- a/solution.py
+++ b/solution.py
@@ -12,7 +12,8 @@
 SPARE = CAP - MAIN
 EX_DEV = 2
 BF, F32, I32 = jnp.bfloat16, jnp.float32, jnp.int32
-VMEM = 60 * 1024 * 1024
+VMEM = 40 * 1024 * 1024
+LONG = pl.CostEstimate(flops=int(4e10), bytes_accessed=int(12e6), transcendentals=0)
 
 
 def block_rows(n):
@@ -38,45 +39,60 @@
     return jnp.where(mask > 0, rank, -1.0)
 
 
-def dispatch(shard_refs, ids, tok_dev):
+def dispatch(shard_refs, ids, tok_dev, after=()):
     n = len(shard_refs)
     rows = block_rows(n)
     d = shard_refs[0][0].shape[1]
+    cols = d // 4
     flat = [a for s in shard_refs for a in s]
     lens = [len(s) for s in shard_refs]
 
     def kernel(ids_ref, *refs):
-        out_ref = refs[-1]
-        eid = [ids_ref[j].astype(F32) for j in range(NJ)]
-        acc, at = None, 0
+        hot_ref, out_ref = refs[-1], refs[-2]
+        shards_of, at = [], 0
         for a in range(n):
-            shard = refs[at : at + lens[a]]
+            shards_of.append(refs[at : at + lens[a]])
             at += lens[a]
-            last = shard[-1]
-            routes = last[last.shape[0] - 16 :, 0:tok_dev].astype(F32)[0:8]
-            keys = expert_keys(routes, eid)
-            parts = []
-            for array in range(2):
-                slots = row_slots(n, a, array).astype(F32)
-                hot = [jnp.where(keys[j : j + 1] == slots, 1.0, 0.0) for j in range(NJ)]
-                parts.append(jnp.concatenate(hot, axis=0))
+
+        @pl.when(pl.program_id(0) == 0)
+        def _():
+            eid = [ids_ref[j].astype(F32) for j in range(NJ)]
+            for a in range(n):
+                last = shards_of[a][-1]
+                routes = last[last.shape[0] - 16 :, 0:tok_dev].astype(F32)[0:8]
+                keys = expert_keys(routes, eid)
+                for array in range(2):
+                    slots = row_slots(n, a, array).astype(F32)
+                    hot = [jnp.where(keys[j : j + 1] == slots, 1.0, 0.0) for j in range(NJ)]
+                    hot = jnp.concatenate(hot, axis=0).astype(BF)
+                    hot_ref[a, :, array * tok_dev : (array + 1) * tok_dev] = hot
+
+        acc = None
+        for a in range(n):
+            shard = shards_of[a]
             if len(shard) == 1:
-                hot = jnp.concatenate(parts, axis=1).astype(BF)
-                got = jnp.dot(hot, shard[0][0 : 2 * tok_dev, :], preferred_element_type=F32)
+                got = jnp.dot(hot_ref[a], shard[0][0 : 2 * tok_dev, :], preferred_element_type=F32)
             else:
-                got = jnp.dot(parts[0].astype(BF), shard[0][...], preferred_element_type=F32)
-                got += jnp.dot(parts[1].astype(BF), shard[1][0:tok_dev, :], preferred_element_type=F32)
+                got = jnp.dot(hot_ref[a, :, 0:tok_dev], shard[0][...], preferred_element_type=F32)
+                got += jnp.dot(
+                    hot_ref[a, :, tok_dev:], shard[1][0:tok_dev, :], preferred_element_type=F32
+                )
             acc = got if acc is None else acc + got
         for j in range(NJ):
             out_ref[j] = acc[j * rows : (j + 1) * rows].astype(BF)
 
     return pl.pallas_call(
         kernel,
+        name="dispatch",
+        grid=(d // cols,),
         out_shape=jax.ShapeDtypeStruct((NJ, rows, d), BF),
-        in_specs=[pl.BlockSpec(memory_space=pltpu.SMEM)] + [pl.BlockSpec(a.shape, lambda: (0, 0)) for a in flat],
-        out_specs=pl.BlockSpec((NJ, rows, d), lambda: (0, 0, 0)),
+        in_specs=[pl.BlockSpec(memory_space=pltpu.SMEM)]
+        + [pl.BlockSpec((a.shape[0], cols), lambda i: (0, i)) for a in flat]
+        + [pl.BlockSpec(memory_space=pl.ANY)] * len(after),
+        out_specs=pl.BlockSpec((NJ, rows, cols), lambda i: (0, 0, i)),
+        scratch_shapes=[pltpu.VMEM((n, NJ * rows, 2 * tok_dev), BF)],
         compiler_params=pltpu.CompilerParams(vmem_limit_bytes=VMEM),
-    )(ids, *flat)
+    )(ids, *flat, *after)
 
 
 def expert(recv, n, w_gate, w_up, w_down, proj_in, proj_out):
@@ -128,6 +144,8 @@
     back_rows = n * (MAIN + 8)
     return pl.pallas_call(
         kernel,
+        name="expert",
+        cost_estimate=LONG,
         grid=(ff // chunk,),
         out_shape=jax.ShapeDtypeStruct((NJ, back_rows, 2 * r), BF),
         in_specs=[
@@ -144,44 +162,69 @@
     )(recv, w_gate, w_up, w_down, proj_in, proj_out)
 
 
-def outer(ids, pieces, routes_t, weight_t, in_model, out_model, member):
-    r = out_model.shape[1] // 2
+def features(tokens, cotangent, proj_in, proj_out):
+    t = tokens.shape[0]
+    r = proj_in.shape[0]
+    contract = (((1,), (1,)), ((), ()))
+
+    def kernel(x_ref, c_ref, pi_ref, po_ref, out_ref):
+        out_ref[:, 0:r] = lax.dot_general(x_ref[...], pi_ref[...], contract, preferred_element_type=F32).astype(BF)
+        out_ref[:, r:] = lax.dot_general(c_ref[...], po_ref[...], contract, preferred_element_type=F32).astype(BF)
+
+    return pl.pallas_call(
+        kernel,
+        name="features",
+        cost_estimate=LONG,
+        out_shape=jax.ShapeDtypeStruct((t, 2 * r), BF),
+        compiler_params=pltpu.CompilerParams(vmem_limit_bytes=VMEM),
+    )(tokens, cotangent, proj_in, proj_out)
+
+
+def outer(ids, pieces, routes_t, weight_t, example, table, into=None):
+    r = table.shape[1] // 2
     part = MAIN + 8
     k = NJ * part
     half = r // 2
 
-    def kernel(ids_ref, routes_ref, weight_ref, im_ref, om_ref, mem_ref, *refs):
-        out_ref = refs[-1]
+    def kernel(ids_ref, routes_ref, weight_ref, ex_ref, table_ref, *refs):
+        refs = refs[: len(pieces)] + refs[len(pieces) + (into is not None) :]
+        if into is None:
+            out_ref = refs[len(pieces)]
+        else:
+            final_ref, out_ref, sem = refs[len(pieces) :]
         routes = routes_ref[...].astype(F32)
         weight = weight_ref[...]
-        table = jnp.concatenate([im_ref[...], om_ref[...], mem_ref[...]], axis=1)
+        example = ex_ref[...].astype(F32)
         lane = lax.broadcasted_iota(I32, (1, 2 * r), 1)
         col = lax.broadcasted_iota(I32, (k, NJ * 2 * r), 1) // (2 * r)
         row = lax.broadcasted_iota(I32, (k, NJ * 2 * r), 0) // part
         own = col == row
         pr = lax.broadcasted_iota(I32, (part, 1), 0)
-        for p, (_, n, shard) in enumerate(pieces):
+        for p, (_, shard) in enumerate(pieces):
             eid = [ids_ref[p * NJ + j] for j in range(NJ)]
             keys = expert_keys(routes, [e.astype(F32) for e in eid])
             q = pr - MAIN - shard * SPARE
             slots = jnp.where(pr < MAIN, pr, jnp.where((q >= 0) & (q < SPARE), MAIN + q, -9)).astype(F32)
-            hot, scale = [], []
+            hot, scale, held, second = [], [], [], []
             for j in range(NJ):
                 h = jnp.where(keys[j : j + 1] == slots, 1.0, 0.0)
                 we = jnp.sum(jnp.where(routes == eid[j].astype(F32), weight, 0.0), axis=0, keepdims=True)
                 hot.append(h)
                 scale.append(jnp.sum(h * we, axis=1, keepdims=True))
+                held.append(jnp.sum(h, axis=1, keepdims=True))
+                second.append(jnp.sum(h * example, axis=1, keepdims=True))
             hot = jnp.concatenate(hot, axis=0).astype(BF)
             scale = jnp.concatenate(scale, axis=0)
-            sel = jnp.dot(hot, table, preferred_element_type=F32)
-            im = sel[:, 0 : 2 * r] * scale
-            om = sel[:, 2 * r : 4 * r] * scale
-            mem = sel[:, 4 * r : 6 * r]
-            ret = refs[p]
-            got = [ret[j, shard * part : (shard + 1) * part, :].astype(F32) for j in range(NJ)]
-            got = jnp.concatenate(got, axis=0)
-            inner = jnp.concatenate([got[:, 0:r], got[:, 0:r]], axis=1) * mem
-            outh = jnp.concatenate([got[:, r:], got[:, r:]], axis=1)
+            held = jnp.concatenate(held, axis=0)
+            second = jnp.concatenate(second, axis=0)
+            mem = jnp.where(lane < r, held - second, second)
+            sel = jnp.dot(hot, table_ref[...], preferred_element_type=F32) * scale
+            got = jnp.concatenate([refs[p][j].astype(F32) for j in range(NJ)], axis=0)
+            twice = lambda v: jnp.concatenate([v, v], axis=1)
+            im = twice(sel[:, 0:r]) * mem
+            om = twice(sel[:, r:])
+            inner = twice(got[:, 0:r]) * mem
+            outh = twice(got[:, r:])
             for g, (left, right) in enumerate(((im, outh), (inner, om))):
                 wide = jnp.concatenate([right] * NJ, axis=1)
                 wide = jnp.where(own, wide, 0.0).astype(BF)
@@ -192,17 +235,43 @@
                     for s in range(EX_DEV):
                         even = res[s * r : s * r + half, j * 2 * r : (j + 1) * 2 * r]
                         odd = res[s * r + half : (s + 1) * r, j * 2 * r : (j + 1) * 2 * r]
-                        out_ref[s, eid[j], g] = jnp.where(lane < r, even, odd).astype(BF)
-
-    arrays = [a for a, _, _ in pieces]
+                        block = jnp.where(lane < r, even, odd).astype(BF)
+                        if into is None:
+                            out_ref[s, eid[j], g] = block
+                        else:
+                            out_ref[s, j, g] = block
+            if into is not None:
+                copies = []
+                for s in range(EX_DEV):
+                    for x in range(NX):
+                        src = out_ref.at[s, pl.ds(x * NC, NC)]
+                        dst = final_ref.at[s, pl.ds(eid[x * NC], NC)]
+                        copies.append(pltpu.make_async_copy(src, dst, sem.at[s * NX + x]))
+                for c in copies:
+                    c.start()
+                for c in copies:
+                    c.wait()
+
+    arrays = [a for a, _ in pieces]
     vmem = pl.BlockSpec(memory_space=pltpu.VMEM)
+    extra, out_specs, scratch, alias = [], vmem, [], {}
+    if into is not None:
+        assert len(pieces) == 1
+        extra, out_specs = [into], pl.BlockSpec(memory_space=pl.ANY)
+        scratch = [pltpu.VMEM((EX_DEV, NJ, 2, half, 2 * r), BF), pltpu.SemaphoreType.DMA((EX_DEV * NX,))]
+        alias = {5 + len(arrays): 0}
     return pl.pallas_call(
         kernel,
+        name="outer",
         out_shape=jax.ShapeDtypeStruct((EX_DEV, NZ * NJ, 2, half, 2 * r), BF),
-        in_specs=[pl.BlockSpec(memory_space=pltpu.SMEM)] + [vmem] * (5 + len(arrays)),
-        out_specs=vmem,
+        in_specs=[pl.BlockSpec(memory_space=pltpu.SMEM)]
+        + [vmem] * (4 + len(arrays))
+        + [pl.BlockSpec(memory_space=pl.ANY)] * len(extra),
+        out_specs=out_specs,
+        scratch_shapes=scratch,
+        input_output_aliases=alias,
         compiler_params=pltpu.CompilerParams(vmem_limit_bytes=VMEM),
-    )(ids, routes_t, weight_t, in_model, out_model, member, *arrays)
+    )(ids, routes_t, weight_t, example, table, *arrays, *extra)
 
 
 def along_z(a, k):
@@ -241,23 +310,27 @@
     top, bottom = along_z(fwd[:split], 1), along_z(back[split:], -1)
     shard_steps.append(([(top, bottom)], [4]))
 
-    pieces, ids = [], []
-    for refs, dist in shard_steps:
-        n = len(refs)
-        got = plane_exchange(dispatch(refs, here, tok_dev))
-        ret = plane_exchange(expert(got, n, wg, wu, wd, proj_in, proj_out))
+    table = features(tokens, cotangent, order(proj_model), proj_model)
+    rets = []
+    for i, (refs, dist) in enumerate(shard_steps):
+        after = rets[i - 2 : i - 1] if i >= 2 else [table] * i
+        got = plane_exchange(dispatch(refs, here, tok_dev, after))
+        rets.append(expert(got, len(refs), wg, wu, wd, proj_in, proj_out))
+
+    part = MAIN + 8
+    most = plane_exchange(jnp.concatenate(rets[:-1], axis=1))
+    last, most = lax.optimization_barrier((rets[-1], most))
+    last = along_z(plane_exchange(last), 4)
+    pieces, at = [], 0
+    for refs, dist in shard_steps[:-1]:
         for a, k in enumerate(dist):
-            pieces.append((ret if k == 0 else along_z(ret, k), n, a))
-            ids.append(plane((z - k) % NZ))
-
-    dot = lambda a, p: lax.dot_general(a, p, (((1,), (1,)), ((), ())), preferred_element_type=F32)
-    in_model = dot(tokens, order(proj_model)).astype(BF)
-    out_model = dot(cotangent, proj_model).astype(BF)
-    lanes = jnp.arange(2 * r, dtype=I32)[None, :] // r
-    member = (example_ids[:, None] == lanes).astype(BF)
-    in_model = jnp.concatenate([in_model, in_model], axis=1) * member
-    out_model = jnp.concatenate([out_model, out_model], axis=1)
-    out = outer(jnp.concatenate(ids), pieces, routes_t, weight_t, in_model, out_model, member)
+            rows = most[:, at : at + part]
+            pieces.append((rows if k == 0 else along_z(rows, k), a))
+            at += part
+    ids = [plane((z - k) % NZ) for _, dist in shard_steps for k in dist]
+    mine = (routes_t, weight_t, example_ids[None, :], table)
+    out = outer(jnp.concatenate(ids[:-1]), pieces, *mine)
+    out = outer(ids[-1], [(last, 0)], *mine, into=out)
     return out.reshape(EX_DEV, NZ * NJ, 2, r * r)
 
 

time: 284 us -> 214 us (0.75)
  waiting for transfers between devices: 114 us -> 45.3 us
  local copies, waits for them, and re-layouts: 15.1 us -> 41.2 us
  starting transfers between devices: 76.7 us -> 61 us
  Pallas kernels: 68.5 us -> 56.7 us
    ppermute x15, waiting for transfers between devices: 82.5 us -> 9.11 us  [along_z(): return lax.ppermute(a, 'z', [(i, (i + k) % NZ) for i in range(NZ)])]
    unnamed x50 -> x80, local copies, waits for them, and re-layouts: 9.77 us -> 32.2 us
    all_to_all x10 -> x7, starting transfers between devices: 51.3 us -> 35.2 us  [plane_exchange(): lax.all_to_all(a, ('x', 'c'), split_axis=0, concat_axis=0, tiled=True)]
    pallas_call x11 -> x13, Pallas kernels: 68.5 us -> 56.7 us  [the longest x5 28.5 us: expert(): pl.pallas_call(kernel, name='expert', cost_estimate=LONG, grid=(ff // chu...]
    slice x4, local copies, waits for them, and re-layouts: 0.43 us -> 5.17 us  [shards(): order = lambda p: jnp.concatenate([p[0::2], p[1::2]], axis=0)]
    all_to_all x10 -> x7, waiting for transfers between devices: 31.7 us -> 36.2 us  [plane_exchange(): lax.all_to_all(a, ('x', 'c'), split_axis=0, concat_axis=0, tiled=True)]
  transfers between devices with their start and end apart: 25 -> 22, of which waited for: 9 -> 7; matrix products, arithmetic and copies ran while one was open for 2% -> 5% of each run, Pallas kernels for 21% -> 26%
where the time goes in v2:
time: 214 us; the launch traced here: 211 us
  starting transfers between devices  61 us (29%)
  Pallas kernels  56.7 us (26%)
  waiting for transfers between devices  45.3 us (21%)
  local copies, waits for them, and re-layouts  41.2 us (19%)
  other arithmetic  6.07 us (3%)
    all_to_all x7, waiting for transfers between devices, plane_exchange(): lax.all_to_all(a, ('x', 'c'), split_axis=0, concat_axis=0, tiled=True)  36.2 us
    all_to_all x7, starting transfers between devices, plane_exchange(): lax.all_to_all(a, ('x', 'c'), split_axis=0, concat_axis=0, tiled=True)  35.2 us
    unnamed x80, local copies, waits for them, and re-layouts  32.2 us
    pallas_call x5, Pallas kernels, expert(): pl.pallas_call(kernel, name='expert', cost_estimate=LONG, grid=(ff // chu...  28.5 us
    ppermute x15, starting transfers between devices, along_z(): return lax.ppermute(a, 'z', [(i, (i + k) % NZ) for i in range(NZ)])  25.8 us
    pallas_call x5, Pallas kernels, dispatch(): pl.pallas_call(kernel, name='dispatch', grid=(d // cols,), out_shape=jax....  21.1 us
    ppermute x15, waiting for transfers between devices, along_z(): return lax.ppermute(a, 'z', [(i, (i + k) % NZ) for i in range(NZ)])  9.11 us
    pallas_call x2, Pallas kernels, outer(): pl.pallas_call(kernel, name='outer', out_shape=jax.ShapeDtypeStruct((EX_D...  6.68 us
  transfers between devices with their start and end apart: 22, of which 7 were waited for; matrix products, arithmetic and copies ran while one was open for 5% of the time, Pallas kernels for 26%

profile of v2, /device:TPU:1, one launch (start us, length us, event | category | flops | bytes accessed | tf_op | source)
XLA Modules:
  0.0 210.7 jit_solution(4767101071817686151)
XLA Ops:
  4.5 4.0 %collective-permute-start.4 = (bf16[272,2048]{1,0:T(8,128)(2,1)S(1)}, bf16[272,2048]{1,0:T(8,128)(2,1)}, u32[]{:S(2)}, u32[]{:S(2)}) collective-permute-start(bf16[272,2048]{1,0:T(8,128)(2,1)S(1)} %fusion.1.refs_0_), channel_id=1, source_target_pairs={{0,14},{2,0},{4,2},{6,4},{8,6},{10,8},{12,10},{14,12},{1,15},{3,1}... | collective-permute-start | bytes 3342344 | tf_op jit(solution)/shard_map/ppermute | solution.py:278
  11.5 5.4 %all-to-all-start = ((bf16[8,40,2048]{2,1,0:T(8,128)(2,1)}), bf16[8,40,2048]{2,1,0:T(8,128)(2,1)S(1)}, u32[]{:S(2)}, u32[]{:S(2)}) async-start(bf16[8,40,2048]{2,1,0:T(8,128)(2,1)} %dispatch.5), calls=%async_computation | async-start | bytes 2621440 | tf_op jit(solution)/shard_map/all_to_all | solution.py:282
  27.6 5.3 %collective-permute-done.refs_0_ = bf16[272,2048]{1,0:T(8,128)(2,1)} collective-permute-done((bf16[272,2048]{1,0:T(8,128)(2,1)S(1)}, bf16[272,2048]{1,0:T(8,128)(2,1)}, u32[]{:S(2)}, u32[]{:S(2)}) %collective-permute-start) | collective-permute-done | bytes 1114144 | tf_op jit(solution)/shard_map/ppermute | solution.py:278
  36.3 5.1 %dispatch.8 = bf16[8,72,2048]{2,1,0:T(8,128)(2,1)} custom-call(s32[8]{0:T(128)S(1)} %add_add_fusion.7.ids_ref, bf16[272,2048]{1,0:T(8,128)(2,1)} %collective-permute-done.refs_0_, bf16[272,2048]{1,0:T(8,128)(2,1)} %collective-permute-done.4.refs_1_, bf16[128,128]{1,0:T(8,128)(2,1)S(1)} %copy-done.5), custom_call_target="tpu_custom_call" | custom-call | tf_op jit(solution)/shard_map/dispatch/pallas_call | solution.py:84
  41.4 6.2 %all-to-all-start.3 = ((bf16[8,72,2048]{2,1,0:T(8,128)(2,1)}), bf16[8,72,2048]{2,1,0:T(8,128)(2,1)}, u32[]{:S(2)}, u32[]{:S(2)}) async-start(bf16[8,72,2048]{2,1,0:T(8,128)(2,1)} %dispatch.8), calls=%async_computation.3 | async-start | bytes 4718592 | tf_op jit(solution)/shard_map/all_to_all | solution.py:282
  53.3 4.1 %expert.5.refs_2_ = bf16[8,24,128]{2,1,0:T(8,128)(2,1)S(1)} custom-call(bf16[8,40,2048]{2,1,0:T(8,128)(2,1)S(1)} %all-to-all-done.x_ref, bf16[2048,768]{1,0:T(8,128)(2,1)S(1)} %bitcast.15, bf16[2048,768]{1,0:T(8,128)(2,1)S(1)} %bitcast.20, bf16[768,2048]{1,0:T(8,128)(2,1)S(1)} %bitcast.25, bf16[64,768]{1,0:T(8,128)(2,1)S(1)} %copy-done.13, ...), custom_call_target="tpu_custom_call" | custom-call | flops 40000000000 | bytes 12000000 | tf_op jit(solution)/shard_map/expert/pallas_call | solution.py:145
  61.9 4.8 %dispatch.6 = bf16[8,72,2048]{2,1,0:T(8,128)(2,1)} custom-call(s32[8]{0:T(128)S(1)} %add_add_fusion.7.ids_ref, bf16[272,2048]{1,0:T(8,128)(2,1)} %collective-permute-done.1.refs_0_, bf16[272,2048]{1,0:T(8,128)(2,1)S(1)} %collective-permute-done.5.refs_1_, bf16[8,24,128]{2,1,0:T(8,128)(2,1)S(1)} %expert.5.refs_2_), custom_call_target="tpu_custom_call" | custom-call | tf_op jit(solution)/shard_map/dispatch/pallas_call | solution.py:84
  67.4 9.5 %all-to-all-done.3.x_ref = bf16[8,72,2048]{2,1,0:T(8,128)(2,1)} async-done(((bf16[8,72,2048]{2,1,0:T(8,128)(2,1)}), bf16[8,72,2048]{2,1,0:T(8,128)(2,1)}, u32[]{:S(2)}, u32[]{:S(2)}) %all-to-all-start.3) | async-done | bytes 2359328 | tf_op jit(solution)/shard_map/all_to_all | solution.py:282
  76.9 5.1 %all-to-all-start.1 = ((bf16[8,72,2048]{2,1,0:T(8,128)(2,1)}), bf16[8,72,2048]{2,1,0:T(8,128)(2,1)}, u32[]{:S(2)}, u32[]{:S(2)}) async-start(bf16[8,72,2048]{2,1,0:T(8,128)(2,1)} %dispatch.6), calls=%async_computation.1 | async-start | bytes 4718592 | tf_op jit(solution)/shard_map/all_to_all | solution.py:282
  88.5 6.6 %expert.8.refs_2_ = bf16[8,48,128]{2,1,0:T(8,128)(2,1)S(1)} custom-call(bf16[8,72,2048]{2,1,0:T(8,128)(2,1)} %all-to-all-done.3.x_ref, bf16[2048,768]{1,0:T(8,128)(2,1)S(1)} %bitcast.16, bf16[2048,768]{1,0:T(8,128)(2,1)S(1)} %bitcast.21, bf16[768,2048]{1,0:T(8,128)(2,1)S(1)} %bitcast.26, bf16[64,768]{1,0:T(8,128)(2,1)S(1)} %copy-done.14, ...), custom_call_target="tpu_custom_call" | custom-call | flops 40000000000 | bytes 12000000 | tf_op jit(solution)/shard_map/expert/pallas_call | solution.py:145
  99.6 4.1 %dispatch.9 = bf16[8,72,2048]{2,1,0:T(8,128)(2,1)} custom-call(s32[8]{0:T(128)S(1)} %add_add_fusion.7.ids_ref, bf16[272,2048]{1,0:T(8,128)(2,1)S(1)} %collective-permute-done.2.refs_0_, bf16[272,2048]{1,0:T(8,128)(2,1)S(1)} %collective-permute-done.6.refs_1_, bf16[8,48,128]{2,1,0:T(8,128)(2,1)S(1)} %expert.8.refs_2_), custom_call_target="tpu_custom_call" | custom-call | tf_op jit(solution)/shard_map/dispatch/pallas_call | solution.py:84
  103.7 7.5 %all-to-all-done.1.x_ref = bf16[8,72,2048]{2,1,0:T(8,128)(2,1)} async-done(((bf16[8,72,2048]{2,1,0:T(8,128)(2,1)}), bf16[8,72,2048]{2,1,0:T(8,128)(2,1)}, u32[]{:S(2)}, u32[]{:S(2)}) %all-to-all-start.1) | async-done | bytes 2359328 | tf_op jit(solution)/shard_map/all_to_all | solution.py:282
  111.2 4.4 %all-to-all-start.4 = ((bf16[8,72,2048]{2,1,0:T(8,128)(2,1)}), bf16[8,72,2048]{2,1,0:T(8,128)(2,1)S(1)}, u32[]{:S(2)}, u32[]{:S(2)}) async-start(bf16[8,72,2048]{2,1,0:T(8,128)(2,1)} %dispatch.9), calls=%async_computation.4 | async-start | bytes 4718592 | tf_op jit(solution)/shard_map/all_to_all | solution.py:282
  121.3 6.6 %expert.6.refs_2_ = bf16[8,48,128]{2,1,0:T(8,128)(2,1)S(1)} custom-call(bf16[8,72,2048]{2,1,0:T(8,128)(2,1)} %all-to-all-done.1.x_ref, bf16[2048,768]{1,0:T(8,128)(2,1)S(1)} %bitcast.17, bf16[2048,768]{1,0:T(8,128)(2,1)S(1)} %bitcast.22, bf16[768,2048]{1,0:T(8,128)(2,1)S(1)} %bitcast.27, bf16[64,768]{1,0:T(8,128)(2,1)S(1)} %copy-done.15, ...), custom_call_target="tpu_custom_call" | custom-call | flops 40000000000 | bytes 12000000 | tf_op jit(solution)/shard_map/expert/pallas_call | solution.py:145
  128.0 4.1 %dispatch.7 = bf16[8,40,2048]{2,1,0:T(8,128)(2,1)} custom-call(s32[8]{0:T(128)S(1)} %add_add_fusion.7.ids_ref, bf16[128,2048]{1,0:T(8,128)(2,1)} %collective-permute-done.3.refs_0_, bf16[144,2048]{1,0:T(8,128)(2,1)S(1)} %collective-permute-done.7.refs_1_, bf16[8,48,128]{2,1,0:T(8,128)(2,1)S(1)} %expert.6.refs_2_), custom_call_target="tpu_custom_call" | custom-call | tf_op jit(solution)/shard_map/dispatch/pallas_call | solution.py:84
  132.1 12.7 %all-to-all-done.4.x_ref = bf16[8,72,2048]{2,1,0:T(8,128)(2,1)S(1)} async-done(((bf16[8,72,2048]{2,1,0:T(8,128)(2,1)}), bf16[8,72,2048]{2,1,0:T(8,128)(2,1)S(1)}, u32[]{:S(2)}, u32[]{:S(2)}) %all-to-all-start.4) | async-done | bytes 2359328 | tf_op jit(solution)/shard_map/all_to_all | solution.py:282
  144.8 5.0 %all-to-all-start.2 = ((bf16[8,40,2048]{2,1,0:T(8,128)(2,1)}), bf16[8,40,2048]{2,1,0:T(8,128)(2,1)}, u32[]{:S(2)}, u32[]{:S(2)}) async-start(bf16[8,40,2048]{2,1,0:T(8,128)(2,1)} %dispatch.7), calls=%async_computation.2 | async-start | bytes 2621440 | tf_op jit(solution)/shard_map/all_to_all | solution.py:282
  155.5 5.1 %expert.9 = bf16[8,48,128]{2,1,0:T(8,128)(2,1)S(1)} custom-call(bf16[8,72,2048]{2,1,0:T(8,128)(2,1)S(1)} %all-to-all-done.4.x_ref, bf16[2048,768]{1,0:T(8,128)(2,1)S(1)} %bitcast.18, bf16[2048,768]{1,0:T(8,128)(2,1)S(1)} %bitcast.23, bf16[768,2048]{1,0:T(8,128)(2,1)S(1)} %bitcast.28, bf16[64,768]{1,0:T(8,128)(2,1)S(1)} %copy-done.15, ...), custom_call_target="tpu_custom_call" | custom-call | flops 40000000000 | bytes 12000000 | tf_op jit(solution)/shard_map/expert/pallas_call | solution.py:145
  161.4 6.5 %all-to-all-done.2.x_ref = bf16[8,40,2048]{2,1,0:T(8,128)(2,1)} async-done(((bf16[8,40,2048]{2,1,0:T(8,128)(2,1)}), bf16[8,40,2048]{2,1,0:T(8,128)(2,1)}, u32[]{:S(2)}, u32[]{:S(2)}) %all-to-all-start.2) | async-done | bytes 1310752 | tf_op jit(solution)/shard_map/all_to_all | solution.py:282
  167.9 4.2 %all-to-all-start.5 = ((bf16[8,168,128]{2,1,0:T(8,128)(2,1)}), bf16[8,168,128]{2,1,0:T(8,128)(2,1)S(1)}, u32[]{:S(2)}, u32[]{:S(2)}) async-start(bf16[8,168,128]{2,1,0:T(8,128)(2,1)} %pad_maximum_fusion), calls=%async_computation.5 | async-start | bytes 688128 | tf_op jit(solution)/shard_map/all_to_all | solution.py:282
  177.8 5.9 %expert.7 = bf16[8,24,128]{2,1,0:T(8,128)(2,1)} custom-call(bf16[8,40,2048]{2,1,0:T(8,128)(2,1)} %all-to-all-done.2.x_ref, bf16[2048,768]{1,0:T(8,128)(2,1)S(1)} %bitcast.19, bf16[2048,768]{1,0:T(8,128)(2,1)S(1)} %bitcast.24, bf16[768,2048]{1,0:T(8,128)(2,1)S(1)} %bitcast.29, bf16[64,768]{1,0:T(8,128)(2,1)S(1)} %copy-done.15, bf16[64,768]{1,0:T(8,128)(2,1)S(1)} %copy-done.12), custom_call_target="tpu_custom_call" | custom-call | flops 40000000000 | bytes 12000000 | tf_op jit(solution)/shard_map/expert/pallas_call | solution.py:145
  183.8 4.8 %all-to-all-start.6 = ((bf16[8,24,128]{2,1,0:T(8,128)(2,1)}), bf16[8,24,128]{2,1,0:T(8,128)(2,1)S(1)}, u32[]{:S(2)}, u32[]{:S(2)}) async-start(bf16[8,24,128]{2,1,0:T(8,128)(2,1)} %expert.7), calls=%async_computation.6 | async-start | bytes 98304 | tf_op jit(solution)/shard_map/all_to_all | solution.py:282
  196.7 3.1 %collective-permute-start.8 = (bf16[8,24,128]{2,1,0:T(8,128)(2,1)S(1)}, bf16[8,24,128]{2,1,0:T(8,128)(2,1)S(1)}, u32[]{:S(2)}, u32[]{:S(2)}) collective-permute-start(bf16[8,24,128]{2,1,0:T(8,128)(2,1)S(1)} %all-to-all-done.6), channel_id=1, source_target_pairs={{0,8},{2,10},{4,12},{6,14},{8,0},{10,2},{12,4},{14,6},{1,9},{3,11}... | collective-permute-start | bytes 147464 | tf_op jit(solution)/shard_map/ppermute | solution.py:278
  202.0 5.0 %outer.2.refs_1_ = bf16[2,64,2,32,128]{4,3,2,1,0:T(8,128)(2,1)S(1)} custom-call(s32[56]{0:T(128)S(1)} %concatenate.19.ids_ref, s32[8,128]{1,0:T(8,128)S(1)} %bitcast.9, f32[8,128]{1,0:T(8,128)S(1)} %bitcast.11, s32[1,128]{1,0:T(1,128)S(1)} %bitcast.13, bf16[128,128]{1,0:T(8,128)(2,1)S(1)} %copy-done.6, bf16[8,24,128]{2,1,0:T(8,128)(2,1)S(1)} %get-tuple-element.15.refs_0_, ...), custom_call_target="tpu_custom_call" | custom-call | tf_op jit(solution)/shard_map/outer/pallas_call | solution.py:263
  (133 shorter events, 74.9 us)
Async XLA Ops:
  2.0 30.9 %collective-permute-start = (bf16[272,2048]{1,0:T(8,128)(2,1)S(1)}, bf16[272,2048]{1,0:T(8,128)(2,1)}, u32[]{:S(2)}, u32[]{:S(2)}) collective-permute-start(bf16[272,2048]{1,0:T(8,128)(2,1)S(1)} %fusion.1.refs_0_), channel_id=1, source_target_pairs={{0,2},{2,4},{4,6},{6,8},{8,10},{10,12},{12,14},{14,0},{1,3},{3,5},... | collective-permute-start | bytes 3342344 | tf_op jit(solution)/shard_map/ppermute | solution.py:278
  4.5 28.3 %collective-permute-start.4 = (bf16[272,2048]{1,0:T(8,128)(2,1)S(1)}, bf16[272,2048]{1,0:T(8,128)(2,1)}, u32[]{:S(2)}, u32[]{:S(2)}) collective-permute-start(bf16[272,2048]{1,0:T(8,128)(2,1)S(1)} %fusion.1.refs_0_), channel_id=1, source_target_pairs={{0,14},{2,0},{4,2},{6,4},{8,6},{10,8},{12,10},{14,12},{1,15},{3,1}... | collective-permute-start | bytes 3342344 | tf_op jit(solution)/shard_map/ppermute | solution.py:278
  11.5 29.8 %all-to-all-start = ((bf16[8,40,2048]{2,1,0:T(8,128)(2,1)}), bf16[8,40,2048]{2,1,0:T(8,128)(2,1)S(1)}, u32[]{:S(2)}, u32[]{:S(2)}) async-start(bf16[8,40,2048]{2,1,0:T(8,128)(2,1)} %dispatch.5), calls=%async_computation | async-start | bytes 2621440 | tf_op jit(solution)/shard_map/all_to_all | solution.py:282
  32.9 26.4 %collective-permute-start.1 = (bf16[272,2048]{1,0:T(8,128)(2,1)}, bf16[272,2048]{1,0:T(8,128)(2,1)}, u32[]{:S(2)}, u32[]{:S(2)}) collective-permute-start(bf16[272,2048]{1,0:T(8,128)(2,1)} %collective-permute-done.refs_0_), channel_id=1, source_target_pairs={{0,2},{2,4},{4,6},{6,8},{8,10},{10,12},{12,14},{14,0},{1,3},{3,5},... | collective-permute-start | bytes 3342344 | tf_op jit(solution)/shard_map/ppermute | solution.py:278
  32.9 26.4 %collective-permute-start.5 = (bf16[272,2048]{1,0:T(8,128)(2,1)}, bf16[272,2048]{1,0:T(8,128)(2,1)S(1)}, u32[]{:S(2)}, u32[]{:S(2)}) collective-permute-start(bf16[272,2048]{1,0:T(8,128)(2,1)} %collective-permute-done.4.refs_1_), channel_id=1, source_target_pairs={{0,14},{2,0},{4,2},{6,4},{8,6},{10,8},{12,10},{14,12},{1,15},{3,1}... | collective-permute-start | bytes 3342344 | tf_op jit(solution)/shard_map/ppermute | solution.py:278
  41.4 35.5 %all-to-all-start.3 = ((bf16[8,72,2048]{2,1,0:T(8,128)(2,1)}), bf16[8,72,2048]{2,1,0:T(8,128)(2,1)}, u32[]{:S(2)}, u32[]{:S(2)}) async-start(bf16[8,72,2048]{2,1,0:T(8,128)(2,1)} %dispatch.8), calls=%async_computation.3 | async-start | bytes 4718592 | tf_op jit(solution)/shard_map/all_to_all | solution.py:282
  59.2 36.0 %collective-permute-start.2 = (bf16[272,2048]{1,0:T(8,128)(2,1)}, bf16[272,2048]{1,0:T(8,128)(2,1)S(1)}, u32[]{:S(2)}, u32[]{:S(2)}) collective-permute-start(bf16[272,2048]{1,0:T(8,128)(2,1)} %collective-permute-done.1.refs_0_), channel_id=1, source_target_pairs={{0,2},{2,4},{4,6},{6,8},{8,10},{10,12},{12,14},{14,0},{1,3},{3,5},... | collective-permute-start | bytes 3342344 | tf_op jit(solution)/shard_map/ppermute | solution.py:278
  59.2 36.9 %collective-permute-start.6 = (bf16[272,2048]{1,0:T(8,128)(2,1)S(1)}, bf16[272,2048]{1,0:T(8,128)(2,1)S(1)}, u32[]{:S(2)}, u32[]{:S(2)}) collective-permute-start(bf16[272,2048]{1,0:T(8,128)(2,1)S(1)} %collective-permute-done.5.refs_1_), channel_id=1, source_target_pairs={{0,14},{2,0},{4,2},{6,4},{8,6},{10,8},{12,10},{14,12},{1,15},{3,1}... | collective-permute-start | bytes 3342344 | tf_op jit(solution)/shard_map/ppermute | solution.py:278
  76.9 34.4 %all-to-all-start.1 = ((bf16[8,72,2048]{2,1,0:T(8,128)(2,1)}), bf16[8,72,2048]{2,1,0:T(8,128)(2,1)}, u32[]{:S(2)}, u32[]{:S(2)}) async-start(bf16[8,72,2048]{2,1,0:T(8,128)(2,1)} %dispatch.6), calls=%async_computation.1 | async-start | bytes 4718592 | tf_op jit(solution)/shard_map/all_to_all | solution.py:282
  96.1 31.9 %collective-permute-start.3 = (bf16[128,2048]{1,0:T(8,128)(2,1)}, bf16[128,2048]{1,0:T(8,128)(2,1)}, u32[]{:S(2)}, u32[]{:S(2)}) collective-permute-start(bf16[128,2048]{1,0:T(8,128)(2,1)} %slice.52), channel_id=1, source_target_pairs={{0,2},{2,4},{4,6},{6,8},{8,10},{10,12},{12,14},{14,0},{1,3},{3,5},... | collective-permute-start | bytes 1572872 | tf_op jit(solution)/shard_map/ppermute | solution.py:278
  96.9 31.0 %collective-permute-start.7 = (bf16[144,2048]{1,0:T(8,128)(2,1)}, bf16[144,2048]{1,0:T(8,128)(2,1)S(1)}, u32[]{:S(2)}, u32[]{:S(2)}) collective-permute-start(bf16[144,2048]{1,0:T(8,128)(2,1)} %slice.53), channel_id=1, source_target_pairs={{0,14},{2,0},{4,2},{6,4},{8,6},{10,8},{12,10},{14,12},{1,15},{3,1}... | collective-permute-start | bytes 1769480 | tf_op jit(solution)/shard_map/ppermute | solution.py:278
  111.2 33.6 %all-to-all-start.4 = ((bf16[8,72,2048]{2,1,0:T(8,128)(2,1)}), bf16[8,72,2048]{2,1,0:T(8,128)(2,1)S(1)}, u32[]{:S(2)}, u32[]{:S(2)}) async-start(bf16[8,72,2048]{2,1,0:T(8,128)(2,1)} %dispatch.9), calls=%async_computation.4 | async-start | bytes 4718592 | tf_op jit(solution)/shard_map/all_to_all | solution.py:282
  144.8 23.1 %all-to-all-start.2 = ((bf16[8,40,2048]{2,1,0:T(8,128)(2,1)}), bf16[8,40,2048]{2,1,0:T(8,128)(2,1)}, u32[]{:S(2)}, u32[]{:S(2)}) async-start(bf16[8,40,2048]{2,1,0:T(8,128)(2,1)} %dispatch.7), calls=%async_computation.2 | async-start | bytes 2621440 | tf_op jit(solution)/shard_map/all_to_all | solution.py:282
  167.9 15.9 %all-to-all-start.5 = ((bf16[8,168,128]{2,1,0:T(8,128)(2,1)}), bf16[8,168,128]{2,1,0:T(8,128)(2,1)S(1)}, u32[]{:S(2)}, u32[]{:S(2)}) async-start(bf16[8,168,128]{2,1,0:T(8,128)(2,1)} %pad_maximum_fusion), calls=%async_computation.5 | async-start | bytes 688128 | tf_op jit(solution)/shard_map/all_to_all | solution.py:282
  177.8 24.2 %copy-start.6 = (bf16[128,128]{1,0:T(8,128)(2,1)S(1)}, bf16[128,128]{1,0:T(8,128)(2,1)}, u32[]{:S(2)}) copy-start(bf16[128,128]{1,0:T(8,128)(2,1)} %copy-done.4) | copy-start | bytes 98308
  177.8 24.2 %copy-start.16 = (s32[128,8]{0,1:T(8,128)S(1)}, s32[128,8]{0,1:T(8,128)}, u32[]{:S(2)}) copy-start(s32[128,8]{0,1:T(8,128)} %param.12) | copy-start | bytes 12292
  183.8 12.9 %all-to-all-start.6 = ((bf16[8,24,128]{2,1,0:T(8,128)(2,1)}), bf16[8,24,128]{2,1,0:T(8,128)(2,1)S(1)}, u32[]{:S(2)}, u32[]{:S(2)}) async-start(bf16[8,24,128]{2,1,0:T(8,128)(2,1)} %expert.7), calls=%async_computation.6 | async-start | bytes 98304 | tf_op jit(solution)/shard_map/all_to_all | solution.py:282
  188.6 6.9 %collective-permute-start.9 = (bf16[8,24,128]{2,1,0:T(8,128)(2,1)S(1)}, bf16[8,24,128]{2,1,0:T(8,128)(2,1)S(1)}, u32[]{:S(2)}, u32[]{:S(2)}) collective-permute-start(bf16[8,24,128]{2,1,0:T(8,128)(2,1)S(1)} %get-tuple-element.14), channel_id=1, source_target_pairs={{0,14},{2,0},{4,2},{6,4},{8,6},{10,8},{12,10},{14,12},{1,15},{3,1}... | collective-permute-start | bytes 147464 | tf_op jit(solution)/shard_map/ppermute | solution.py:278
  188.9 7.7 %collective-permute-start.10 = (bf16[8,24,128]{2,1,0:T(8,128)(2,1)S(1)}, bf16[8,24,128]{2,1,0:T(8,128)(2,1)S(1)}, u32[]{:S(2)}, u32[]{:S(2)}) collective-permute-start(bf16[8,24,128]{2,1,0:T(8,128)(2,1)S(1)} %get-tuple-element.13), channel_id=1, source_target_pairs={{0,2},{2,4},{4,6},{6,8},{8,10},{10,12},{12,14},{14,0},{1,3},{3,5},... | collective-permute-start | bytes 147464 | tf_op jit(solution)/shard_map/ppermute | solution.py:278
  190.2 9.8 %collective-permute-start.11 = (bf16[8,24,128]{2,1,0:T(8,128)(2,1)S(1)}, bf16[8,24,128]{2,1,0:T(8,128)(2,1)S(1)}, u32[]{:S(2)}, u32[]{:S(2)}) collective-permute-start(bf16[8,24,128]{2,1,0:T(8,128)(2,1)S(1)} %get-tuple-element.12), channel_id=1, source_target_pairs={{0,12},{2,14},{4,0},{6,2},{8,4},{10,6},{12,8},{14,10},{1,13},{3,15... | collective-permute-start | bytes 147464 | tf_op jit(solution)/shard_map/ppermute | solution.py:278
  190.9 9.1 %collective-permute-start.12 = (bf16[8,24,128]{2,1,0:T(8,128)(2,1)S(1)}, bf16[8,24,128]{2,1,0:T(8,128)(2,1)S(1)}, u32[]{:S(2)}, u32[]{:S(2)}) collective-permute-start(bf16[8,24,128]{2,1,0:T(8,128)(2,1)S(1)} %get-tuple-element.11), channel_id=1, source_target_pairs={{0,4},{2,6},{4,8},{6,10},{8,12},{10,14},{12,0},{14,2},{1,5},{3,7},... | collective-permute-start | bytes 147464 | tf_op jit(solution)/shard_map/ppermute | solution.py:278
  192.5 7.4 %collective-permute-start.13 = (bf16[8,24,128]{2,1,0:T(8,128)(2,1)S(1)}, bf16[8,24,128]{2,1,0:T(8,128)(2,1)S(1)}, u32[]{:S(2)}, u32[]{:S(2)}) collective-permute-start(bf16[8,24,128]{2,1,0:T(8,128)(2,1)S(1)} %get-tuple-element.10), channel_id=1, source_target_pairs={{0,10},{2,12},{4,14},{6,0},{8,2},{10,4},{12,6},{14,8},{1,11},{3,13... | collective-permute-start | bytes 147464 | tf_op jit(solution)/shard_map/ppermute | solution.py:278
  195.5 6.5 %collective-permute-start.14 = (bf16[8,24,128]{2,1,0:T(8,128)(2,1)S(1)}, bf16[8,24,128]{2,1,0:T(8,128)(2,1)S(1)}, u32[]{:S(2)}, u32[]{:S(2)}) collective-permute-start(bf16[8,24,128]{2,1,0:T(8,128)(2,1)S(1)} %get-tuple-element.9), channel_id=1, source_target_pairs={{0,6},{2,8},{4,10},{6,12},{8,14},{10,0},{12,2},{14,4},{1,7},{3,9},... | collective-permute-start | bytes 147464 | tf_op jit(solution)/shard_map/ppermute | solution.py:278
  196.7 10.3 %collective-permute-start.8 = (bf16[8,24,128]{2,1,0:T(8,128)(2,1)S(1)}, bf16[8,24,128]{2,1,0:T(8,128)(2,1)S(1)}, u32[]{:S(2)}, u32[]{:S(2)}) collective-permute-start(bf16[8,24,128]{2,1,0:T(8,128)(2,1)S(1)} %all-to-all-done.6), channel_id=1, source_target_pairs={{0,8},{2,10},{4,12},{6,14},{8,0},{10,2},{12,4},{14,6},{1,9},{3,11}... | collective-permute-start | bytes 147464 | tf_op jit(solution)/shard_map/ppermute | solution.py:278
  (38 other events, 302.2 us)
